TPU v7x, 256 devices: a whole 4x4x8 slice. The times are simulated.
256 devices in a mesh: surf: 16 (over y, x), hist: 16 (over z, core).
Axes of the slice: x: 4, y: 4, z: 8, core: 2. Of those that a mesh axis runs over, the one named last changes fastest.
Arguments:
- excitation: float32 [2, 64, 8192], P(None, None, 'surf'), may hold values from -6 to 6
- history: bfloat16 [128, 64, 8192], P('hist', None, 'surf'), may hold values from -6 to 6
- blocks: bfloat16 [128, 64, 8, 128, 128], P('hist', 'surf'), may hold values from -0.015625 to 0.015625
- pattern: int32 [128, 64, 8], P('hist', 'surf'), may hold values from 0 to 63, as said below
- near_inverse: float32 [64, 128, 128], P('surf')
Outputs:
- currents: float32 [2, 64, 8192], P(None, None, 'surf')
Inputs may be any that keep to these rules, and one draw needn't show every extreme that they name: `pattern`: slot 0 of every history step and row block names that row block itself; every other slot names a column block drawn independently and evenly for each history step, row block and slot.
All inputs are finite; a program needn't handle non-finite values.
Results may differ from a plain program's by a relative error of at most 0.0003.
Values may be sent and summed in bfloat16 or wider, within the bound.
No kernel may reach another device: no remote copies, remote signals or barrier semaphores. Data moves between devices by JAX's collectives and lax.ppermute only.
A program may use at most 128 MiB of HBM per device.

v0:
```python
import jax
import jax.numpy as jnp
from jax import lax
from jax.sharding import PartitionSpec as P


def shifted(array, axis, by):
    length = lax.axis_size(axis)
    pairs = [(i, i + by) for i in range(length) if 0 <= i + by < length]
    return lax.ppermute(array, axis, pairs)


def gather_history(slab):
    return lax.all_gather(slab, "surf", axis=2, tiled=True)


def retarded(blocks, pattern, gathered):
    steps, channels, panels = gathered.shape
    block_size = blocks.shape[3]
    hist_blocks = gathered.reshape(steps, channels, panels // block_size, block_size)
    picked = jax.vmap(lambda slab, cols: slab[:, cols])(hist_blocks, pattern)
    return jnp.einsum("kisab,krisb->ria", blocks, picked, preferred_element_type=jnp.float32)


def near_solve(near_inverse, field):
    out = jnp.einsum("iab,rib->ria", near_inverse, field, precision=lax.Precision.HIGHEST)
    return out.reshape(out.shape[0], -1)


def solve_step(partial_value, excite_now, near_inverse):
    channels, row_blocks, block_size = partial_value.shape
    summed = lax.psum(partial_value, "hist")
    field = excite_now.reshape(channels, row_blocks, block_size) - summed
    return near_solve(near_inverse, field)


def local(excitation, history, blocks, pattern, near_inverse):
    gathered_one = gather_history(history)
    first = solve_step(retarded(blocks, pattern, gathered_one), excitation[0], near_inverse)
    first_low = first.astype(jnp.bfloat16)
    at_front = lax.axis_index("hist") == 0
    carried = shifted(history[-1], "hist", 1)
    front = jnp.where(at_front, first_low, carried)
    gathered_two = gather_history(jnp.concatenate([front[None], history[:-1]], axis=0))
    second = solve_step(retarded(blocks, pattern, gathered_two), excitation[1], near_inverse)
    return jnp.stack([first, second])


def solution(mesh):
    in_specs = (
        P(None, None, "surf"),
        P("hist", None, "surf"),
        P("hist", "surf", None, None, None),
        P("hist", "surf", None),
        P("surf", None, None),
    )
    out_specs = P(None, None, "surf")
    return jax.shard_map(local, mesh=mesh, in_specs=in_specs, out_specs=out_specs, check_vma=False)
```

profile of v0, /device:TPU:1, one launch (start us, length us, event | category | flops | bytes accessed | tf_op | source)
XLA Modules:
  0.0 454.5 jit_solution(11175734275502833820)
XLA Ops:
  6.5 0.0 copy-start
  6.5 0.0 all-gather.3.cloned.1.call-start
  6.5 0.7 all-gather.3.cloned.1.call-update
  7.3 0.0 all-reduce.3.cloned.1.call-start
  7.3 0.8 slice_bitcast_fusion
  8.2 4.9 %collective-permute-start = (bf16[64,512]{1,0:T(8,128)(2,1)S(1)}, bf16[64,512]{1,0:T(8,128)(2,1)S(1)}, u32[]{:S(2)}, u32[]{:S(2)}) collective-permute-start(bf16[64,512]{1,0:T(8,128)(2,1)S(1)} %slice_bitcast_fusion), channel_id=1, source_target_pairs={{0,1},{1,2},{2,3},{3,4},{4,5},{5,6},{6,7},{7,8},{8,9},{9,10},{10,1... | collective-permute-start | bytes 196616 | tf_op jit(solution)/shard_map/ppermute | solution.py:10
  13.1 0.7 fusion.4
  13.8 0.1 reshape.10
  13.9 82.2 %all-gather.3.cloned.1.call-done = bf16[8,64,8192]{2,1,0:T(8,128)(2,1)} async-done(((bf16[8,64,512]{2,1,0:T(8,128)(2,1)}), bf16[8,64,8192]{2,1,0:T(8,128)(2,1)}) %all-gather.3.cloned.1.call-update) | async-done | bytes 8388624 | tf_op jit(solution)/shard_map/all_gather | solution.py:14
  96.1 9.0 %copy_bitcast_fusion.1 = bf16[8,64,64,128]{3,1,2,0:T(8,128)(2,1)} fusion(bf16[8,64,8192]{2,1,0:T(8,128)(2,1)} %all-gather.3.cloned.1.call-done), kind=kLoop, calls=%fused_computation.3 | loop fusion | bytes 16777216 | tf_op jit(solution)/shard_map/reshape | solution.py:20
  105.1 6.7 %gather_fusion = bf16[256,64,128]{2,1,0:T(8,128)(2,1)} fusion(bf16[8,64,64,128]{3,1,2,0:T(8,128)(2,1)} %copy_bitcast_fusion.1, s32[256]{0:T(256)S(1)} %reshape.10), kind=kCustom, calls=%fused_computation | custom fusion | bytes 8390656 | tf_op jit(solution)/shard_map/vmap()/gather | solution.py:21
  111.8 0.0 copy-start.2
  111.8 0.0 copy-start.1
  111.8 8.3 %convolution_bitcast_fusion.3 = f32[64,4,128]{2,0,1:T(8,128)} fusion(bf16[8,64,4,8,128]{4,1,3,2,0:T(8,128)(2,1)} %bitcast.56, bf16[8,4,8,128,128]{4,3,2,1,0:T(8,128)(2,1)} %param.7), kind=kOutput, calls=%fused_computation.7 | convolution fusion | flops 536870912 | bytes 12713984 | tf_op jit(solution)/shard_map/kisab,krisb->ria/dot_general | solution.py:22
  120.1 0.0 all-reduce.3.cloned.1.call-update
  120.2 0.0 all-gather.5.cloned.1.call-start
  120.2 0.0 copy-done.2
  120.3 0.0 copy-done.1
  120.4 107.7 %all-reduce.3.cloned.1.call-done = f32[64,4,128]{2,0,1:T(8,128)} async-done(((f32[64,4,128]{2,0,1:T(8,128)}), f32[64,4,128]{2,0,1:T(8,128)}) %all-reduce.3.cloned.1.call-update) | async-done | bytes 131088 | tf_op jit(solution)/shard_map/psum | solution.py:32
  228.1 0.0 copy-done
  228.1 1.5 convolution_bitcast_fusion.2
  229.6 0.0 collective-permute-done
  229.7 0.9 pad_maximum_fusion
  230.5 0.0 all-gather.5.cloned.1.call-update
  230.5 0.0 all-reduce.5.cloned.1.call-start
  230.6 83.1 %all-gather.5.cloned.1.call-done = bf16[8,64,8192]{2,1,0:T(8,128)(2,1)} async-done(((bf16[8,64,512]{2,1,0:T(8,128)(2,1)}), bf16[8,64,8192]{2,1,0:T(8,128)(2,1)}) %all-gather.5.cloned.1.call-update) | async-done | bytes 8388624 | tf_op jit(solution)/shard_map/all_gather | solution.py:14
  313.7 9.0 %copy_bitcast_fusion = bf16[8,64,64,128]{3,1,2,0:T(8,128)(2,1)} fusion(bf16[8,64,8192]{2,1,0:T(8,128)(2,1)} %all-gather.5.cloned.1.call-done), kind=kLoop, calls=%fused_computation.2 | loop fusion | bytes 16777216 | tf_op jit(solution)/shard_map/reshape | solution.py:20
  322.7 6.7 %gather_fusion.1 = bf16[256,64,128]{2,1,0:T(8,128)(2,1)} fusion(bf16[8,64,64,128]{3,1,2,0:T(8,128)(2,1)} %copy_bitcast_fusion, s32[256]{0:T(256)S(1)} %reshape.10), kind=kCustom, calls=%fused_computation.1 | custom fusion | bytes 8390656 | tf_op jit(solution)/shard_map/vmap()/gather | solution.py:21
  329.4 8.3 %convolution_bitcast_fusion.1 = f32[64,4,128]{2,0,1:T(8,128)} fusion(bf16[8,64,4,8,128]{4,1,3,2,0:T(8,128)(2,1)} %bitcast.55, bf16[8,4,8,128,128]{4,3,2,1,0:T(8,128)(2,1)} %param.7), kind=kOutput, calls=%fused_computation.5 | convolution fusion | flops 536870912 | bytes 12713984 | tf_op jit(solution)/shard_map/kisab,krisb->ria/dot_general | solution.py:22
  337.7 0.0 all-reduce.5.cloned.1.call-update
  337.7 0.1 copy.20
  337.8 0.1 stack_reshape.6
  337.9 107.7 %all-reduce.5.cloned.1.call-done = f32[64,4,128]{2,0,1:T(8,128)} async-done(((f32[64,4,128]{2,0,1:T(8,128)}), f32[64,4,128]{2,0,1:T(8,128)}) %all-reduce.5.cloned.1.call-update) | async-done | bytes 131088 | tf_op jit(solution)/shard_map/psum | solution.py:32
  445.6 1.5 convolution_bitcast_fusion
  447.1 0.1 copy.24
  447.2 0.1 stack_reshape.7
  447.3 0.7 pad_maximum_fusion.1
  (5 shorter events, 0.2 us)
Async XLA Ops:
  6.5 221.6 %copy-start = (f32[4,128,128]{2,1,0:T(8,128)S(1)}, f32[4,128,128]{2,1,0:T(8,128)}, u32[]{:S(2)}) copy-start(f32[4,128,128]{2,1,0:T(8,128)} %param.9) | copy-start | bytes 786436
  6.5 89.6 %all-gather.3.cloned.1.call-start = ((), (), s32[]{:S(2)}) async-start(), calls=%async_computation | async-start | bytes 8912896 | tf_op jit(solution)/shard_map/all_gather | solution.py:14
  7.3 220.8 %all-reduce.3.cloned.1.call-start = ((), (), s32[]{:S(2)}) async-start(), calls=%async_computation.1 | async-start | bytes 262144 | tf_op jit(solution)/shard_map/psum | solution.py:32
  8.2 221.5 %collective-permute-start = (bf16[64,512]{1,0:T(8,128)(2,1)S(1)}, bf16[64,512]{1,0:T(8,128)(2,1)S(1)}, u32[]{:S(2)}, u32[]{:S(2)}) collective-permute-start(bf16[64,512]{1,0:T(8,128)(2,1)S(1)} %slice_bitcast_fusion), channel_id=1, source_target_pairs={{0,1},{1,2},{2,3},{3,4},{4,5},{5,6},{6,7},{7,8},{8,9},{9,10},{10,1... | collective-permute-start | bytes 196616 | tf_op jit(solution)/shard_map/ppermute | solution.py:10
  111.8 8.4 %copy-start.2 = (f32[2,64,512]{2,1,0:T(8,128)S(1)}, f32[2,64,512]{2,1,0:T(8,128)}, u32[]{:S(2)}) copy-start(f32[2,64,512]{2,1,0:T(8,128)} %param.5) | copy-start | bytes 786436
  111.8 8.4 %copy-start.1 = (bf16[8,64,512]{2,1,0:T(8,128)(2,1)S(1)}, bf16[8,64,512]{2,1,0:T(8,128)(2,1)}, u32[]{:S(2)}) copy-start(bf16[8,64,512]{2,1,0:T(8,128)(2,1)} %param.6) | copy-start | bytes 1572868
  120.2 193.5 %all-gather.5.cloned.1.call-start = ((), (), s32[]{:S(2)}) async-start(), calls=%async_computation.2 | async-start | bytes 8912896 | tf_op jit(solution)/shard_map/all_gather | solution.py:14
  230.5 215.1 %all-reduce.5.cloned.1.call-start = ((), (), s32[]{:S(2)}) async-start(), calls=%async_computation.3 | async-start | bytes 262144 | tf_op jit(solution)/shard_map/psum | solution.py:32
Sparse Core Ops, SparseCore 0:
  9.8 86.2 all-gather.2
  120.3 107.7 all-reduce.2
  230.8 82.8 all-gather.4
  337.8 107.7 all-reduce.4
where the time goes:
time: 455 us
  waiting for transfers between devices  381 us (84%)
  local copies, waits for them, and re-layouts  32.9 us (7%)
  matrix products  19.6 us (4%)
  between operations  13.3 us (3%)
  starting transfers between devices  5.05 us (1%)
    psum x2, waiting for transfers between devices, solve_step(): summed = lax.psum(partial_value, 'hist')  215 us
    all_gather x2, waiting for transfers between devices, gather_history(): return lax.all_gather(slab, 'surf', axis=2, tiled=True)  165 us
    reshape x2, local copies, waits for them, and re-layouts, retarded(): gathered.reshape(steps, channels, panels // block_size, block_size)  18 us
    dot_general x2, matrix products, retarded(): jnp.einsum('kisab,krisb->ria', blocks, picked, preferred_element_type=jnp...  16.6 us
    gather x3, local copies, waits for them, and re-layouts, retarded(): picked = jax.vmap(lambda slab, cols: slab[:, cols])(hist_blocks, pattern)  13.5 us
  transfers between devices with their start and end apart: 5, of which 4 were waited for; matrix products, arithmetic and copies ran while one was open for 6% of the time, Pallas kernels for 0%

commit v1 on v0

v1 whole, which is shorter than its diff:
```python
import jax
import jax.numpy as jnp
from jax import lax
from jax.experimental import pallas as pl
from jax.experimental.pallas import tpu as pltpu
from jax.sharding import Mesh
from jax.sharding import PartitionSpec as P

F32 = jnp.float32
BF16 = jnp.bfloat16
Y, X, Z, C = 4, 4, 8, 2
STEPS, ROWS, SLOTS, BS = 8, 4, 8, 128
CH = 64
CHZ = CH // Z
HALF = STEPS // 2
NT = (((1,), (1,)), ((), ()))
VMEM_LIMIT = 56 * 1024 * 1024


def turn(array, axis, by):
    length = lax.axis_size(axis)
    return lax.ppermute(array, axis, [(i, (i + by) % length) for i in range(length)])


def swap_cores(array):
    return lax.ppermute(array, "core", [(0, 1), (1, 0)])


def ring(array, axis):
    half = array.shape[0] // 2
    below = turn(array, axis, 1)
    above = turn(array, axis, -1)
    far_low = turn(below[:half], axis, 1)
    far_high = turn(above[half:], axis, -1)
    return jnp.concatenate([array, below, above, far_low, far_high], axis=0)


def gather_history(history):
    first, second = history[:HALF], history[HALF:]
    return jnp.concatenate([ring(ring(first, "x"), "y"), ring(ring(second, "y"), "x")], axis=0)


def entries(cols, steps):
    place = jnp.array([0, 1, 3, 2], jnp.int32)
    dy = place[(lax.axis_index("y") - cols // (X * ROWS)) % Y]
    dx = place[(lax.axis_index("x") - (cols // ROWS) % X) % X]
    early = (dy * X + dx) * HALF + steps
    late = Y * X * HALF + (dx * Y + dy) * HALF + steps - HALF
    return jnp.where(steps < HALF, early, late) * ROWS + cols % ROWS


def field_kernel(now_idx, past_idx, blocks_ref, next_ref, table_ref, out_ref, acc):
    k = pl.program_id(0)

    def slab(code):
        lane = pl.multiple_of(lax.rem(code, ROWS) * BS, BS)
        return table_ref[lax.div(code, ROWS), :, pl.ds(lane, BS)]

    def gathered(idx, row):
        base = (k * ROWS + row) * SLOTS
        return jnp.concatenate([slab(idx[base + s]) for s in range(SLOTS)], axis=1)

    def matrix(ref, lead, row):
        return jnp.concatenate([ref[lead + (row, s)] for s in range(SLOTS)], axis=1)

    @pl.when(k == 0)
    def _():
        for row in range(ROWS):
            first = lax.dot_general(gathered(now_idx, row), matrix(blocks_ref, (0,), row), NT, preferred_element_type=F32)
            last = []
            for s in range(SLOTS):
                last.append(slab(past_idx[row * SLOTS + s]))
            second = lax.dot_general(jnp.concatenate(last, axis=1), matrix(next_ref, (), row), NT, preferred_element_type=F32)
            acc[row, :CH] = first
            acc[row, CH:] = second

    @pl.when(k > 0)
    def _():
        for row in range(ROWS):
            both = jnp.concatenate([gathered(now_idx, row), gathered(past_idx, row)], axis=0)
            acc[row] += lax.dot_general(both, matrix(blocks_ref, (0,), row), NT, preferred_element_type=F32)

    @pl.when(k == STEPS - 1)
    def _():
        for row in range(ROWS):
            for f in range(2):
                for z in range(Z):
                    start = f * CH + z * CHZ
                    out_ref[row // 2, z, row % 2, f] = acc[row, start : start + CHZ]


def field_partials(blocks, following, table, now_idx, past_idx):
    return pl.pallas_call(
        field_kernel,
        grid_spec=pltpu.PrefetchScalarGridSpec(
            num_scalar_prefetch=2,
            grid=(STEPS,),
            in_specs=[
                pl.BlockSpec((1, ROWS, SLOTS, BS, BS), lambda k, a, b: (k, 0, 0, 0, 0)),
                pl.BlockSpec(memory_space=pltpu.VMEM),
                pl.BlockSpec(memory_space=pltpu.VMEM),
            ],
            out_specs=pl.BlockSpec(memory_space=pltpu.VMEM),
            scratch_shapes=[pltpu.VMEM((ROWS, 2 * CH, BS), F32)],
        ),
        out_shape=jax.ShapeDtypeStruct((2, Z, 2, 2, CHZ, BS), F32),
        compiler_params=pltpu.CompilerParams(vmem_limit_bytes=VMEM_LIMIT),
        name="retarded_partials",
    )(now_idx, past_idx, blocks, following, table)


def exact_dot(a, b):
    return lax.dot_general(a, b, NT, precision=lax.Precision.HIGHEST, preferred_element_type=F32)


def first_kernel(parts_ref, excite_ref, near_ref, current_ref, low_ref, rest_ref):
    total = parts_ref[0]
    for z in range(1, Z):
        total = total + parts_ref[z]
    solved = []
    for row in range(2):
        at = row * 2 * CHZ
        field = excite_ref[0, row] - total[at : at + CHZ]
        solved.append(exact_dot(field, near_ref[row]))
        rest_ref[row] = excite_ref[1, row] - total[at + CHZ : at + 2 * CHZ]
    both = jnp.concatenate(solved, axis=0)
    current_ref[...] = both
    low = both.astype(BF16)
    for s in range(Y * X):
        low_ref[s] = low


def first_solve(parts, excite, near):
    return pl.pallas_call(
        first_kernel,
        out_shape=(
            jax.ShapeDtypeStruct((2 * CHZ, BS), F32),
            jax.ShapeDtypeStruct((Y * X, 2 * CHZ, BS), BF16),
            jax.ShapeDtypeStruct((2, CHZ, BS), F32),
        ),
        name="first_solve",
    )(parts, excite, near)


def second_kernel(idx, mine_ref, other_ref, blocks_ref, rest_ref, near_ref, current_ref, out_ref, table):
    for h, ref in enumerate((mine_ref, other_ref)):
        for s in range(Y * X):
            wide = ref[s].astype(F32)
            for row in range(2):
                table[(h * Y * X + s) * 2 + row] = wide[row * CHZ : (row + 1) * CHZ]
    solved = []
    for row in range(2):
        picked = [table[idx[row * SLOTS + s]].astype(BF16) for s in range(SLOTS)]
        matrix = jnp.concatenate([blocks_ref[(row * SLOTS + s) * BS : (row * SLOTS + s + 1) * BS] for s in range(SLOTS)], axis=1)
        term = lax.dot_general(jnp.concatenate(picked, axis=1), matrix, NT, preferred_element_type=F32)
        solved.append(exact_dot(rest_ref[row] - term, near_ref[row]))
    second = jnp.concatenate(solved, axis=0)
    first = current_ref[...]
    for z in range(Z):
        out_ref[z, 0] = first
        out_ref[z, 1] = second


def second_solve(idx, mine, other, blocks, rest, near, current):
    return pl.pallas_call(
        second_kernel,
        in_specs=[pl.BlockSpec(memory_space=pltpu.SMEM)] + [pl.BlockSpec(memory_space=pltpu.VMEM)] * 6,
        out_specs=pl.BlockSpec(memory_space=pltpu.VMEM),
        out_shape=jax.ShapeDtypeStruct((Z, 2, 2 * CHZ, BS), F32),
        scratch_shapes=[pltpu.VMEM((2 * Y * X * 2, CHZ, BS), F32)],
        name="second_solve",
    )(idx, mine, other, blocks, rest, near, current)


def spread_front(blocks, pattern):
    core, z = lax.axis_index("core"), lax.axis_index("z")
    size = 2 * SLOTS * BS
    codes = jnp.broadcast_to(pattern[0].astype(BF16).reshape(2, 1, 2 * SLOTS), (2, 16, 2 * SLOTS))
    codes = jnp.pad(codes, ((0, 0), (0, 0), (0, BS - 2 * SLOTS)))
    packs = jnp.concatenate([blocks[0].reshape(2, size, BS), codes], axis=1)
    sent = lax.ppermute(packs[1], "core", [(0, 1)])
    held = jnp.where(core == 0, packs[0], sent)
    held = jnp.where(z % 8 == 4, lax.ppermute(held, "z", [(0, 4)]), held)
    held = jnp.where(z % 4 == 2, lax.ppermute(held, "z", [(0, 2), (4, 6)]), held)
    held = jnp.where(z % 2 == 1, lax.ppermute(held, "z", [(0, 1), (2, 3), (4, 5), (6, 7)]), held)
    return held, held[size, : 2 * SLOTS].astype(jnp.int32)


def local(excitation, history, blocks, pattern, near_inverse):
    core, z = lax.axis_index("core"), lax.axis_index("z")
    bands = lax.axis_size(("z", "core"))
    back = [(i + 1, i) for i in range(bands - 1)]
    following = lax.ppermute(blocks[0], ("z", "core"), back)
    following_pattern = lax.ppermute(pattern[0], ("z", "core"), back)
    table = gather_history(history)
    front, front_pattern = spread_front(blocks, pattern)

    steps = jnp.arange(STEPS, dtype=jnp.int32)[:, None, None]
    now_idx = entries(pattern, steps)
    past_idx = jnp.concatenate(
        [entries(following_pattern, jnp.int32(STEPS - 1))[None], entries(pattern, steps - 1)[1:]], axis=0
    )
    partial = field_partials(blocks, following, table, now_idx.reshape(-1), past_idx.reshape(-1))

    kept = lax.dynamic_index_in_dim(partial, core, 0, keepdims=False)
    given = lax.dynamic_index_in_dim(partial, 1 - core, 0, keepdims=False)
    pair = (kept + swap_cores(given)).reshape(Z, 4 * CHZ, BS)
    parts = lax.all_to_all(pair, "z", 0, 0)

    excite = lax.dynamic_slice(excitation, (0, z * CHZ, core * 2 * BS), (2, CHZ, 2 * BS))
    excite = excite.reshape(2, CHZ, 2, BS).transpose(0, 2, 1, 3)
    near = lax.dynamic_slice(near_inverse, (core * 2, 0, 0), (2, BS, BS))
    current, low, rest = first_solve(parts, excite, near)

    mine = lax.all_to_all(low, ("y", "x"), 0, 0)
    other = swap_cores(mine)
    block_core = (front_pattern % ROWS) // 2
    front_idx = ((block_core ^ core) * Y * X + front_pattern // ROWS) * 2 + front_pattern % 2
    ready = second_solve(front_idx, mine, other, front, rest, near, current)

    kept = lax.all_to_all(ready, "z", 0, 0)
    given = swap_cores(kept)
    both = jnp.stack([jnp.where(core == 0, kept, given), jnp.where(core == 0, given, kept)])
    both = both.reshape(C, Z, 2, 2, CHZ, BS)
    return both.transpose(2, 1, 4, 0, 3, 5).reshape(2, CH, ROWS * BS)


def solution(mesh):
    split = Mesh(mesh.devices.reshape(Y, X, Z, C), ("y", "x", "z", "core"))
    surf, hist = ("y", "x"), ("z", "core")
    in_specs = (
        P(None, None, surf),
        P(hist, None, surf),
        P(hist, surf, None, None, None),
        P(hist, surf, None),
        P(surf, None, None),
    )
    out_specs = P(None, None, surf)
    return jax.shard_map(local, mesh=split, in_specs=in_specs, out_specs=out_specs, check_vma=False)
```

time: 455 us -> 203 us (0.45)
  waiting for transfers between devices: 381 us -> 66.5 us
  starting transfers between devices: 5.05 us -> 58.9 us
  matrix products: 19.6 us -> 0 us
  Pallas kernels: 0 us -> 16.9 us
  between operations: 13.3 us -> 0.35 us
  blocking collectives: 0 us -> 11.6 us
  local copies, waits for them, and re-layouts: 32.9 us -> 41.1 us
    psum x2 -> x0, waiting for transfers between devices: 215 us -> none  [solve_step(): summed = lax.psum(partial_value, 'hist')]
    all_gather x2 -> x0, waiting for transfers between devices: 165 us -> none  [gather_history(): return lax.all_gather(slab, 'surf', axis=2, tiled=True)]
    ppermute x1 -> x25, waiting for transfers between devices: 0.01 us -> 51.1 us  [the longest x16 49.8 us: turn(): lax.ppermute(array, axis, [(i, (i + by) % length) for i in range(length)])]
    ppermute x1 -> x25, starting transfers between devices: 4.92 us -> 46.5 us  [the longest x16 20 us: turn(): lax.ppermute(array, axis, [(i, (i + by) % length) for i in range(length)])]
    unnamed x6 -> x29, local copies, waits for them, and re-layouts: 0.01 us -> 20.7 us
    dot_general x4 -> x0, matrix products: 19.6 us -> none  [the longest x2 16.6 us: retarded(): jnp.einsum('kisab,krisb->ria', blocks, picked, preferred_element_type=jnp...]
    pallas_call x0 -> x3, Pallas kernels: none -> 16.9 us  [the longest x1 12.4 us: field_partials(): pl.pallas_call(field_kernel, grid_spec=pltpu.PrefetchScalarGridSpec(num_s...]
    reshape x2, local copies, waits for them, and re-layouts: 18 us -> 1.27 us  [the longest x1 0.64 us: local(): past_idx.reshape(-1)]
  transfers between devices with their start and end apart: 5 -> 27, of which waited for: 4 -> 9; matrix products, arithmetic and copies ran while one was open for 6% -> 21% of each run, Pallas kernels for 0% -> 7%
where the time goes in v1:
time: 203 us; the launch traced here: 202 us
  waiting for transfers between devices  66.5 us (33%)
  starting transfers between devices  58.9 us (29%)
  local copies, waits for them, and re-layouts  41.1 us (20%)
  Pallas kernels  16.9 us (8%)
  blocking collectives  11.6 us (6%)
  other arithmetic  6.15 us (3%)
    ppermute x16, waiting for transfers between devices, turn(): lax.ppermute(array, axis, [(i, (i + by) % length) for i in range(length)])  49.8 us
    unnamed x29, local copies, waits for them, and re-layouts  20.7 us
    ppermute x16, starting transfers between devices, turn(): lax.ppermute(array, axis, [(i, (i + by) % length) for i in range(length)])  20 us
    pallas_call x1, Pallas kernels, field_partials(): pl.pallas_call(field_kernel, grid_spec=pltpu.PrefetchScalarGridSpec(num_s...  12.4 us
    all_to_all x1, blocking collectives, local(): kept = lax.all_to_all(ready, 'z', 0, 0)  11.6 us
    all_to_all x1, waiting for transfers between devices, local(): parts = lax.all_to_all(pair, 'z', 0, 0)  9.06 us
    all_to_all x1, starting transfers between devices, local(): parts = lax.all_to_all(pair, 'z', 0, 0)  8.19 us
    ppermute x3, starting transfers between devices, swap_cores(): return lax.ppermute(array, 'core', [(0, 1), (1, 0)])  6.97 us
  transfers between devices with their start and end apart: 27, of which 9 were waited for; matrix products, arithmetic and copies ran while one was open for 21% of the time, Pallas kernels for 7%

profile of v1, /device:TPU:1, one launch (start us, length us, event | category | flops | bytes accessed | tf_op | source)
XLA Modules:
  0.0 201.6 jit_solution(1196281403956309606)
XLA Ops:
  0.0 2.1 %constant_dynamic-update-slice_fusion.9 = (bf16[16,64,512]{2,1,0:T(8,128)(2,1)}, bf16[16,64,512]{2,1,0:T(8,128)(2,1)}, bf16[128,64,512]{2,1,0:T(8,128)(2,1)}, bf...) fusion(bf16[8,64,512]{2,1,0:T(8,128)(2,1)} %param.9), kind=kLoop, calls=%fused_computation.27 | loop fusion | bytes 1835008
  2.1 2.0 %collective-permute-start.6 = (bf16[4,64,512]{2,1,0:T(8,128)(2,1)S(1)}, bf16[4,64,512]{2,1,0:T(8,128)(2,1)S(1)}, u32[]{:S(2)}, u32[]{:S(2)}) collective-permute-start(bf16[4,64,512]{2,1,0:T(8,128)(2,1)S(1)} %get-tuple-element.20), channel_id=1, source_target_pairs={{0,16},{16,32},{32,48},{48,0},{1,17},{17,33},{33,49},{49,1},{2,18}... | collective-permute-start | bytes 786440 | tf_op jit(solution)/shard_map/ppermute | solution.py:22
  4.1 1.3 collective-permute-start.7
  5.4 1.5 collective-permute-start.14
  6.9 1.4 collective-permute-start.15
  9.0 5.4 %collective-permute-start.4 = (s32[4,8]{1,0:T(4,128)S(1)}, s32[4,8]{1,0:T(4,128)S(1)}, u32[]{:S(2)}, u32[]{:S(2)}) collective-permute-start(s32[4,8]{1,0:T(4,128)S(1)} %get-tuple-element.39), channel_id=1, source_target_pairs={{1,0},{2,1},{3,2},{4,3},{5,4},{6,5},{7,6},{8,7},{9,8},{10,9},{11,1... | collective-permute-start | bytes 392 | tf_op jit(solution)/shard_map/ppermute | solution.py:194
  15.5 1.9 gather_fusion
  17.5 1.9 gather_fusion.1
  20.5 2.6 %slice_bitcast_fusion.4 = (bf16[4,8,128,128]{3,2,1,0:T(8,128)(2,1)}, bf16[1,4,8,128,128]{4,3,2,1,0:T(8,128)(2,1)S(1)}) fusion(bf16[8,4,8,128,128]{4,3,2,1,0:T(8,128)(2,1)} %blocks_ref.1), kind=kLoop, calls=%fused_computation.138 | loop fusion | bytes 3145728 | tf_op jit(solution)/shard_map/squeeze | solution.py:193
  23.2 2.7 %collective-permute-start.9 = (bf16[2,64,512]{2,1,0:T(8,128)(2,1)S(1)}, bf16[2,64,512]{2,1,0:T(8,128)(2,1)S(1)}, u32[]{:S(2)}, u32[]{:S(2)}) collective-permute-start(bf16[2,64,512]{2,1,0:T(8,128)(2,1)S(1)} %slice.83), channel_id=1, source_target_pairs={{0,48},{16,0},{32,16},{48,32},{1,49},{17,1},{33,17},{49,33},{2,50}... | collective-permute-start | bytes 393224 | tf_op jit(solution)/shard_map/ppermute | solution.py:22
  27.7 1.9 collective-permute-done.8
  31.1 2.7 %collective-permute-start.11 = (bf16[16,64,512]{2,1,0:T(8,128)(2,1)}, bf16[16,64,512]{2,1,0:T(8,128)(2,1)S(1)}, u32[]{:S(2)}, u32[]{:S(2)}) collective-permute-start(bf16[16,64,512]{2,1,0:T(8,128)(2,1)} %get-tuple-element.35), channel_id=1, source_target_pairs={{0,192},{64,0},{128,64},{192,128},{1,193},{65,1},{129,65},{193,129... | collective-permute-start | bytes 3145736 | tf_op jit(solution)/shard_map/ppermute | solution.py:22
  34.7 22.2 %collective-permute-done.10 = bf16[16,64,512]{2,1,0:T(8,128)(2,1)S(1)} collective-permute-done((bf16[16,64,512]{2,1,0:T(8,128)(2,1)}, bf16[16,64,512]{2,1,0:T(8,128)(2,1)S(1)}, u32[]{:S(2)}, u32[]{:S(2)}) %collective-permute-start.10) | collective-permute-done | bytes 1048608 | tf_op jit(solution)/shard_map/ppermute | solution.py:22
  56.8 3.1 %collective-permute-start.5 = (bf16[4,8,128,128]{3,2,1,0:T(8,128)(2,1)}, bf16[4,8,128,128]{3,2,1,0:T(8,128)(2,1)}, u32[]{:S(2)}, u32[]{:S(2)}) collective-permute-start(bf16[4,8,128,128]{3,2,1,0:T(8,128)(2,1)} %get-tuple-element.14), channel_id=1, source_target_pairs={{1,0},{2,1},{3,2},{4,3},{5,4},{6,5},{7,6},{8,7},{9,8},{10,9},{11,1... | collective-permute-start | bytes 3145736 | tf_op jit(solution)/shard_map/ppermute | solution.py:193
  61.7 2.7 %collective-permute-start.13 = (bf16[8,64,512]{2,1,0:T(8,128)(2,1)}, bf16[8,64,512]{2,1,0:T(8,128)(2,1)}, u32[]{:S(2)}, u32[]{:S(2)}) collective-permute-start(bf16[8,64,512]{2,1,0:T(8,128)(2,1)} %slice.85), channel_id=1, source_target_pairs={{0,192},{64,0},{128,64},{192,128},{1,193},{65,1},{129,65},{193,129... | collective-permute-start | bytes 1572872 | tf_op jit(solution)/shard_map/ppermute | solution.py:22
  66.0 1.3 collective-permute-start
  69.2 1.1 constant_dynamic-update-slice_fusion.22
  70.3 1.1 constant_dynamic-update-slice_fusion.21
  71.4 4.8 %collective-permute-done.12 = bf16[8,64,512]{2,1,0:T(8,128)(2,1)} collective-permute-done((bf16[8,64,512]{2,1,0:T(8,128)(2,1)}, bf16[8,64,512]{2,1,0:T(8,128)(2,1)}, u32[]{:S(2)}, u32[]{:S(2)}) %collective-permute-start.12) | collective-permute-done | bytes 524320 | tf_op jit(solution)/shard_map/ppermute | solution.py:22
  76.2 1.9 constant_dynamic-update-slice_fusion.20
  78.0 1.9 constant_dynamic-update-slice_fusion.19
  79.9 1.7 constant_dynamic-update-slice_fusion.18
  81.6 1.8 constant_dynamic-update-slice_fusion.8
  83.4 1.8 constant_dynamic-update-slice_fusion.7
  86.7 2.7 %collective-permute-start.19 = (bf16[16,64,512]{2,1,0:T(8,128)(2,1)}, bf16[16,64,512]{2,1,0:T(8,128)(2,1)S(1)}, u32[]{:S(2)}, u32[]{:S(2)}) collective-permute-start(bf16[16,64,512]{2,1,0:T(8,128)(2,1)} %get-tuple-element.31), channel_id=1, source_target_pairs={{0,48},{16,0},{32,16},{48,32},{1,49},{17,1},{33,17},{49,33},{2,50}... | collective-permute-start | bytes 3145736 | tf_op jit(solution)/shard_map/ppermute | solution.py:22
  90.2 6.7 %collective-permute-start.1 = (bf16[2064,128]{1,0:T(8,128)(2,1)}, bf16[2064,128]{1,0:T(8,128)(2,1)S(1)}, u32[]{:S(2)}, u32[]{:S(2)}) collective-permute-start(bf16[2064,128]{1,0:T(8,128)(2,1)} %fusion.2), channel_id=1, source_target_pairs={{0,8},{1,9},{16,24},{17,25},{32,40},{33,41},{48,56},{49,57},{64,72... | collective-permute-start | bytes 1585160 | tf_op jit(solution)/shard_map/ppermute | solution.py:183
  97.7 15.0 %collective-permute-done.18 = bf16[16,64,512]{2,1,0:T(8,128)(2,1)S(1)} collective-permute-done((bf16[16,64,512]{2,1,0:T(8,128)(2,1)}, bf16[16,64,512]{2,1,0:T(8,128)(2,1)S(1)}, u32[]{:S(2)}, u32[]{:S(2)}) %collective-permute-start.18) | collective-permute-done | bytes 1048608 | tf_op jit(solution)/shard_map/ppermute | solution.py:22
  112.9 2.7 %collective-permute-start.21 = (bf16[8,64,512]{2,1,0:T(8,128)(2,1)S(1)}, bf16[8,64,512]{2,1,0:T(8,128)(2,1)S(1)}, u32[]{:S(2)}, u32[]{:S(2)}) collective-permute-start(bf16[8,64,512]{2,1,0:T(8,128)(2,1)S(1)} %slice.89), channel_id=1, source_target_pairs={{0,48},{16,0},{32,16},{48,32},{1,49},{17,1},{33,17},{49,33},{2,50}... | collective-permute-start | bytes 1572872 | tf_op jit(solution)/shard_map/ppermute | solution.py:22
  115.6 1.1 broadcast_select_fusion
  116.7 1.7 collective-permute-start.2
  118.4 1.1 constant_dynamic-update-slice_fusion.13
  119.5 1.1 constant_dynamic-update-slice_fusion.12
  120.6 5.9 %collective-permute-done.20 = bf16[8,64,512]{2,1,0:T(8,128)(2,1)S(1)} collective-permute-done((bf16[8,64,512]{2,1,0:T(8,128)(2,1)S(1)}, bf16[8,64,512]{2,1,0:T(8,128)(2,1)S(1)}, u32[]{:S(2)}, u32[]{:S(2)}) %collective-permute-start.20) | collective-permute-done | bytes 524320 | tf_op jit(solution)/shard_map/ppermute | solution.py:22
  128.2 12.4 %retarded_partials.1 = f32[2,8,2,2,8,128]{5,4,3,2,1,0:T(8,128)} custom-call(s32[256]{0:T(256)} %reshape.42.now_idx, s32[256]{0:T(256)} %reshape.43.past_idx, bf16[8,4,8,128,128]{4,3,2,1,0:T(8,128)(2,1)} %blocks_ref.1, bf16[4,8,128,128]{3,2,1,0:T(8,128)(2,1)} %collective-permute-done.5.next_ref, ...), custom_call_target="tpu_custom_call" | custom-call | tf_op jit(solution)/shard_map/retarded_partials/pallas_call | solution.py:93
  141.5 2.0 collective-permute-start.22
  143.6 1.3 collective-permute-start.3
  144.9 1.6 bitcast_add_fusion
  146.5 8.2 %all-to-all-start = ((f32[8,32,128]{2,1,0:T(8,128)}), f32[8,32,128]{2,1,0:T(8,128)S(1)}, u32[]{:S(2)}, u32[]{:S(2)}) async-start(f32[8,32,128]{2,1,0:T(8,128)} %bitcast.10), calls=%async_computation | async-start | bytes 262144 | tf_op jit(solution)/shard_map/all_to_all | solution.py:208
  154.7 1.3 dynamic-slice_bitcast_fusion.1.excite_ref
  156.7 9.1 %all-to-all-done.parts_ref = f32[8,32,128]{2,1,0:T(8,128)S(1)} async-done(((f32[8,32,128]{2,1,0:T(8,128)}), f32[8,32,128]{2,1,0:T(8,128)S(1)}, u32[]{:S(2)}, u32[]{:S(2)}) %all-to-all-start) | async-done | bytes 131104 | tf_op jit(solution)/shard_map/all_to_all | solution.py:208
  166.4 1.9 first_solve.1
  168.3 4.3 %all-to-all-start.1 = ((bf16[16,16,128]{2,1,0:T(8,128)(2,1)}), bf16[16,16,128]{2,1,0:T(8,128)(2,1)S(1)}, u32[]{:S(2)}, u32[]{:S(2)}) async-start(bf16[16,16,128]{2,1,0:T(8,128)(2,1)} %get-tuple-element.8), calls=%async_computation.1 | async-start | bytes 131072 | tf_op jit(solution)/shard_map/all_to_all | solution.py:215
  172.7 6.4 %all-to-all-done.1.mine_ref = bf16[16,16,128]{2,1,0:T(8,128)(2,1)S(1)} async-done(((bf16[16,16,128]{2,1,0:T(8,128)(2,1)}), bf16[16,16,128]{2,1,0:T(8,128)(2,1)S(1)}, u32[]{:S(2)}, u32[]{:S(2)}) %all-to-all-start.1) | async-done | bytes 65568 | tf_op jit(solution)/shard_map/all_to_all | solution.py:215
  179.1 2.9 %collective-permute-start.23 = (bf16[16,16,128]{2,1,0:T(8,128)(2,1)S(1)}, bf16[16,16,128]{2,1,0:T(8,128)(2,1)S(1)}, u32[]{:S(2)}, u32[]{:S(2)}) collective-permute-start(bf16[16,16,128]{2,1,0:T(8,128)(2,1)S(1)} %all-to-all-done.1.mine_ref), channel_id=1, source_target_pairs={{0,1},{1,0},{2,3},{3,2},{4,5},{5,4},{6,7},{7,6},{8,9},{9,8},{10,11... | collective-permute-start | bytes 196616 | tf_op jit(solution)/shard_map/ppermute | solution.py:26
  183.5 2.6 %second_solve.1 = f32[8,2,16,128]{3,2,1,0:T(8,128)} custom-call(s32[16]{0:T(128)} %fusion.20.idx, bf16[16,16,128]{2,1,0:T(8,128)(2,1)} %copy-done.4, bf16[16,16,128]{2,1,0:T(8,128)(2,1)} %copy-done.6, bf16[2064,128]{1,0:T(8,128)(2,1)} %copy-done.2, f32[2,8,128]{2,1,0:T(8,128)} %get-tuple-element.9.rest_ref, ...), custom_call_target="tpu_custom_call" | custom-call | tf_op jit(solution)/shard_map/second_solve/pallas_call | solution.py:165
  186.1 11.6 %all_to_all.15 = f32[8,2,16,128]{3,2,1,0:T(8,128)S(1)} all-to-all(f32[8,2,16,128]{3,2,1,0:T(8,128)} %second_solve.1), channel_id=1, replica_groups=mesh['y'=4,'x'=4,'z'=8,'core'=2] {'z'}, dimensions={0} | all-to-all | bytes 262144 | tf_op jit(solution)/shard_map/all_to_all | solution.py:221
  197.7 2.1 %collective-permute-start.24 = (f32[8,2,16,128]{3,2,1,0:T(8,128)S(1)}, f32[8,2,16,128]{3,2,1,0:T(8,128)S(1)}, u32[]{:S(2)}, u32[]{:S(2)}) collective-permute-start(f32[8,2,16,128]{3,2,1,0:T(8,128)S(1)} %all_to_all.15), channel_id=1, source_target_pairs={{0,1},{1,0},{2,3},{3,2},{4,5},{5,4},{6,7},{7,6},{8,9},{9,8},{10,11... | collective-permute-start | bytes 393224 | tf_op jit(solution)/shard_map/ppermute | solution.py:26
  199.8 1.0 collective-permute-done.24
  (95 shorter events, 22.1 us)
Async XLA Ops:
  0.0 156.0 %copy-start = (f32[4,128,128]{2,1,0:T(8,128)S(1)}, f32[4,128,128]{2,1,0:T(8,128)}, u32[]{:S(2)}) copy-start(f32[4,128,128]{2,1,0:T(8,128)} %param.12) | copy-start | bytes 786436
  0.0 15.5 %copy-start.1 = (s32[4]{0:T(128)S(1)}, s32[4]{0:T(128)}, u32[]{:S(2)}) copy-start(s32[4]{0:T(128)} %constant.222.clone) | copy-start | bytes 52
  2.1 21.0 %collective-permute-start.6 = (bf16[4,64,512]{2,1,0:T(8,128)(2,1)S(1)}, bf16[4,64,512]{2,1,0:T(8,128)(2,1)S(1)}, u32[]{:S(2)}, u32[]{:S(2)}) collective-permute-start(bf16[4,64,512]{2,1,0:T(8,128)(2,1)S(1)} %get-tuple-element.20), channel_id=1, source_target_pairs={{0,16},{16,32},{32,48},{48,0},{1,17},{17,33},{33,49},{49,1},{2,18}... | collective-permute-start | bytes 786440 | tf_op jit(solution)/shard_map/ppermute | solution.py:22
  4.1 19.1 %collective-permute-start.7 = (bf16[4,64,512]{2,1,0:T(8,128)(2,1)S(1)}, bf16[4,64,512]{2,1,0:T(8,128)(2,1)S(1)}, u32[]{:S(2)}, u32[]{:S(2)}) collective-permute-start(bf16[4,64,512]{2,1,0:T(8,128)(2,1)S(1)} %get-tuple-element.20), channel_id=1, source_target_pairs={{0,48},{16,0},{32,16},{48,32},{1,49},{17,1},{33,17},{49,33},{2,50}... | collective-permute-start | bytes 786440 | tf_op jit(solution)/shard_map/ppermute | solution.py:22
  5.4 60.6 %collective-permute-start.14 = (bf16[4,64,512]{2,1,0:T(8,128)(2,1)}, bf16[4,64,512]{2,1,0:T(8,128)(2,1)}, u32[]{:S(2)}, u32[]{:S(2)}) collective-permute-start(bf16[4,64,512]{2,1,0:T(8,128)(2,1)} %get-tuple-element.19), channel_id=1, source_target_pairs={{0,64},{64,128},{128,192},{192,0},{1,65},{65,129},{129,193},{193,1... | collective-permute-start | bytes 786440 | tf_op jit(solution)/shard_map/ppermute | solution.py:22
  6.9 61.3 %collective-permute-start.15 = (bf16[4,64,512]{2,1,0:T(8,128)(2,1)}, bf16[4,64,512]{2,1,0:T(8,128)(2,1)}, u32[]{:S(2)}, u32[]{:S(2)}) collective-permute-start(bf16[4,64,512]{2,1,0:T(8,128)(2,1)} %get-tuple-element.19), channel_id=1, source_target_pairs={{0,192},{64,0},{128,64},{192,128},{1,193},{65,1},{129,65},{193,129... | collective-permute-start | bytes 786440 | tf_op jit(solution)/shard_map/ppermute | solution.py:22
  9.0 52.7 %collective-permute-start.4 = (s32[4,8]{1,0:T(4,128)S(1)}, s32[4,8]{1,0:T(4,128)S(1)}, u32[]{:S(2)}, u32[]{:S(2)}) collective-permute-start(s32[4,8]{1,0:T(4,128)S(1)} %get-tuple-element.39), channel_id=1, source_target_pairs={{1,0},{2,1},{3,2},{4,3},{5,4},{6,5},{7,6},{8,7},{9,8},{10,9},{11,1... | collective-permute-start | bytes 392 | tf_op jit(solution)/shard_map/ppermute | solution.py:194
  17.5 2.1 %copy-start.5 = (s32[8,4,8]{2,1,0:T(4,128)S(1)}, s32[8,4,8]{2,1,0:T(4,128)}, u32[]{:S(2)}) copy-start(s32[8,4,8]{2,1,0:T(4,128)} %param.11) | copy-start | bytes 3076
  23.1 6.5 %collective-permute-start.8 = (bf16[2,64,512]{2,1,0:T(8,128)(2,1)S(1)}, bf16[2,64,512]{2,1,0:T(8,128)(2,1)S(1)}, u32[]{:S(2)}, u32[]{:S(2)}) collective-permute-start(bf16[2,64,512]{2,1,0:T(8,128)(2,1)S(1)} %slice.82), channel_id=1, source_target_pairs={{0,16},{16,32},{32,48},{48,0},{1,17},{17,33},{33,49},{49,1},{2,18}... | collective-permute-start | bytes 393224 | tf_op jit(solution)/shard_map/ppermute | solution.py:22
  23.2 7.1 %collective-permute-start.9 = (bf16[2,64,512]{2,1,0:T(8,128)(2,1)S(1)}, bf16[2,64,512]{2,1,0:T(8,128)(2,1)S(1)}, u32[]{:S(2)}, u32[]{:S(2)}) collective-permute-start(bf16[2,64,512]{2,1,0:T(8,128)(2,1)S(1)} %slice.83), channel_id=1, source_target_pairs={{0,48},{16,0},{32,16},{48,32},{1,49},{17,1},{33,17},{49,33},{2,50}... | collective-permute-start | bytes 393224 | tf_op jit(solution)/shard_map/ppermute | solution.py:22
  31.1 25.8 %collective-permute-start.10 = (bf16[16,64,512]{2,1,0:T(8,128)(2,1)}, bf16[16,64,512]{2,1,0:T(8,128)(2,1)S(1)}, u32[]{:S(2)}, u32[]{:S(2)}) collective-permute-start(bf16[16,64,512]{2,1,0:T(8,128)(2,1)} %get-tuple-element.35), channel_id=1, source_target_pairs={{0,64},{64,128},{128,192},{192,0},{1,65},{65,129},{129,193},{193,1... | collective-permute-start | bytes 3145736 | tf_op jit(solution)/shard_map/ppermute | solution.py:22
  31.1 29.8 %collective-permute-start.11 = (bf16[16,64,512]{2,1,0:T(8,128)(2,1)}, bf16[16,64,512]{2,1,0:T(8,128)(2,1)S(1)}, u32[]{:S(2)}, u32[]{:S(2)}) collective-permute-start(bf16[16,64,512]{2,1,0:T(8,128)(2,1)} %get-tuple-element.35), channel_id=1, source_target_pairs={{0,192},{64,0},{128,64},{192,128},{1,193},{65,1},{129,65},{193,129... | collective-permute-start | bytes 3145736 | tf_op jit(solution)/shard_map/ppermute | solution.py:22
  56.8 71.4 %collective-permute-start.5 = (bf16[4,8,128,128]{3,2,1,0:T(8,128)(2,1)}, bf16[4,8,128,128]{3,2,1,0:T(8,128)(2,1)}, u32[]{:S(2)}, u32[]{:S(2)}) collective-permute-start(bf16[4,8,128,128]{3,2,1,0:T(8,128)(2,1)} %get-tuple-element.14), channel_id=1, source_target_pairs={{1,0},{2,1},{3,2},{4,3},{5,4},{6,5},{7,6},{8,7},{9,8},{10,9},{11,1... | collective-permute-start | bytes 3145736 | tf_op jit(solution)/shard_map/ppermute | solution.py:193
  60.8 15.4 %collective-permute-start.12 = (bf16[8,64,512]{2,1,0:T(8,128)(2,1)}, bf16[8,64,512]{2,1,0:T(8,128)(2,1)}, u32[]{:S(2)}, u32[]{:S(2)}) collective-permute-start(bf16[8,64,512]{2,1,0:T(8,128)(2,1)} %slice.84), channel_id=1, source_target_pairs={{0,64},{64,128},{128,192},{192,0},{1,65},{65,129},{129,193},{193,1... | collective-permute-start | bytes 1572872 | tf_op jit(solution)/shard_map/ppermute | solution.py:22
  61.7 16.3 %collective-permute-start.13 = (bf16[8,64,512]{2,1,0:T(8,128)(2,1)}, bf16[8,64,512]{2,1,0:T(8,128)(2,1)}, u32[]{:S(2)}, u32[]{:S(2)}) collective-permute-start(bf16[8,64,512]{2,1,0:T(8,128)(2,1)} %slice.85), channel_id=1, source_target_pairs={{0,192},{64,0},{128,64},{192,128},{1,193},{65,1},{129,65},{193,129... | collective-permute-start | bytes 1572872 | tf_op jit(solution)/shard_map/ppermute | solution.py:22
  66.0 23.4 %collective-permute-start = (bf16[2064,128]{1,0:T(8,128)(2,1)}, bf16[2064,128]{1,0:T(8,128)(2,1)S(1)}, u32[]{:S(2)}, u32[]{:S(2)}) collective-permute-start(bf16[2064,128]{1,0:T(8,128)(2,1)} %slice_bitcast_fusion), channel_id=1, source_target_pairs={{0,1},{2,3},{4,5},{6,7},{8,9},{10,11},{12,13},{14,15},{16,17},{18,... | collective-permute-start | bytes 1585160 | tf_op jit(solution)/shard_map/ppermute | solution.py:181
  68.2 17.0 %collective-permute-start.16 = (bf16[2,64,512]{2,1,0:T(8,128)(2,1)S(1)}, bf16[2,64,512]{2,1,0:T(8,128)(2,1)S(1)}, u32[]{:S(2)}, u32[]{:S(2)}) collective-permute-start(bf16[2,64,512]{2,1,0:T(8,128)(2,1)S(1)} %slice.86), channel_id=1, source_target_pairs={{0,64},{64,128},{128,192},{192,0},{1,65},{65,129},{129,193},{193,1... | collective-permute-start | bytes 393224 | tf_op jit(solution)/shard_map/ppermute | solution.py:22
  76.2 9.8 %collective-permute-start.17 = (bf16[2,64,512]{2,1,0:T(8,128)(2,1)S(1)}, bf16[2,64,512]{2,1,0:T(8,128)(2,1)S(1)}, u32[]{:S(2)}, u32[]{:S(2)}) collective-permute-start(bf16[2,64,512]{2,1,0:T(8,128)(2,1)S(1)} %slice.87), channel_id=1, source_target_pairs={{0,192},{64,0},{128,64},{192,128},{1,193},{65,1},{129,65},{193,129... | collective-permute-start | bytes 393224 | tf_op jit(solution)/shard_map/ppermute | solution.py:22
  86.7 26.0 %collective-permute-start.18 = (bf16[16,64,512]{2,1,0:T(8,128)(2,1)}, bf16[16,64,512]{2,1,0:T(8,128)(2,1)S(1)}, u32[]{:S(2)}, u32[]{:S(2)}) collective-permute-start(bf16[16,64,512]{2,1,0:T(8,128)(2,1)} %get-tuple-element.31), channel_id=1, source_target_pairs={{0,16},{16,32},{32,48},{48,0},{1,17},{17,33},{33,49},{49,1},{2,18}... | collective-permute-start | bytes 3145736 | tf_op jit(solution)/shard_map/ppermute | solution.py:22
  86.7 26.1 %collective-permute-start.19 = (bf16[16,64,512]{2,1,0:T(8,128)(2,1)}, bf16[16,64,512]{2,1,0:T(8,128)(2,1)S(1)}, u32[]{:S(2)}, u32[]{:S(2)}) collective-permute-start(bf16[16,64,512]{2,1,0:T(8,128)(2,1)} %get-tuple-element.31), channel_id=1, source_target_pairs={{0,48},{16,0},{32,16},{48,32},{1,49},{17,1},{33,17},{49,33},{2,50}... | collective-permute-start | bytes 3145736 | tf_op jit(solution)/shard_map/ppermute | solution.py:22
  90.2 25.4 %collective-permute-start.1 = (bf16[2064,128]{1,0:T(8,128)(2,1)}, bf16[2064,128]{1,0:T(8,128)(2,1)S(1)}, u32[]{:S(2)}, u32[]{:S(2)}) collective-permute-start(bf16[2064,128]{1,0:T(8,128)(2,1)} %fusion.2), channel_id=1, source_target_pairs={{0,8},{1,9},{16,24},{17,25},{32,40},{33,41},{48,56},{49,57},{64,72... | collective-permute-start | bytes 1585160 | tf_op jit(solution)/shard_map/ppermute | solution.py:183
  112.7 13.7 %collective-permute-start.20 = (bf16[8,64,512]{2,1,0:T(8,128)(2,1)S(1)}, bf16[8,64,512]{2,1,0:T(8,128)(2,1)S(1)}, u32[]{:S(2)}, u32[]{:S(2)}) collective-permute-start(bf16[8,64,512]{2,1,0:T(8,128)(2,1)S(1)} %slice.88), channel_id=1, source_target_pairs={{0,16},{16,32},{32,48},{48,0},{1,17},{17,33},{33,49},{49,1},{2,18}... | collective-permute-start | bytes 1572872 | tf_op jit(solution)/shard_map/ppermute | solution.py:22
  112.9 14.5 %collective-permute-start.21 = (bf16[8,64,512]{2,1,0:T(8,128)(2,1)S(1)}, bf16[8,64,512]{2,1,0:T(8,128)(2,1)S(1)}, u32[]{:S(2)}, u32[]{:S(2)}) collective-permute-start(bf16[8,64,512]{2,1,0:T(8,128)(2,1)S(1)} %slice.89), channel_id=1, source_target_pairs={{0,48},{16,0},{32,16},{48,32},{1,49},{17,1},{33,17},{49,33},{2,50}... | collective-permute-start | bytes 1572872 | tf_op jit(solution)/shard_map/ppermute | solution.py:22
  116.7 26.8 %collective-permute-start.2 = (bf16[2064,128]{1,0:T(8,128)(2,1)S(1)}, bf16[2064,128]{1,0:T(8,128)(2,1)S(1)}, u32[]{:S(2)}, u32[]{:S(2)}) collective-permute-start(bf16[2064,128]{1,0:T(8,128)(2,1)S(1)} %broadcast_select_fusion), channel_id=1, source_target_pairs={{0,4},{8,12},{1,5},{9,13},{16,20},{24,28},{17,21},{25,29},{32,36},... | collective-permute-start | bytes 1585160 | tf_op jit(solution)/shard_map/ppermute | solution.py:184
  141.5 3.4 %collective-permute-start.22 = (f32[8,2,2,8,128]{4,3,2,1,0:T(8,128)S(1)}, f32[8,2,2,8,128]{4,3,2,1,0:T(8,128)S(1)}, u32[]{:S(2)}, u32[]{:S(2)}) collective-permute-start(f32[8,2,2,8,128]{4,3,2,1,0:T(8,128)S(1)} %dynamic-slice_bitcast_fusion), channel_id=1, source_target_pairs={{0,1},{1,0},{2,3},{3,2},{4,5},{5,4},{6,7},{7,6},{8,9},{9,8},{10,11... | collective-permute-start | bytes 393224 | tf_op jit(solution)/shard_map/ppermute | solution.py:26
  143.6 29.0 %collective-permute-start.3 = (bf16[2064,128]{1,0:T(8,128)(2,1)S(1)}, bf16[2064,128]{1,0:T(8,128)(2,1)S(1)}, u32[]{:S(2)}, u32[]{:S(2)}) collective-permute-start(bf16[2064,128]{1,0:T(8,128)(2,1)S(1)} %broadcast_select_fusion.1), channel_id=1, source_target_pairs={{0,2},{4,6},{8,10},{12,14},{1,3},{5,7},{9,11},{13,15},{16,18},{20,... | collective-permute-start | bytes 1585160 | tf_op jit(solution)/shard_map/ppermute | solution.py:185
  146.5 19.2 %all-to-all-start = ((f32[8,32,128]{2,1,0:T(8,128)}), f32[8,32,128]{2,1,0:T(8,128)S(1)}, u32[]{:S(2)}, u32[]{:S(2)}) async-start(f32[8,32,128]{2,1,0:T(8,128)} %bitcast.10), calls=%async_computation | async-start | bytes 262144 | tf_op jit(solution)/shard_map/all_to_all | solution.py:208
  165.7 0.7 copy-start.3
  168.3 10.8 %all-to-all-start.1 = ((bf16[16,16,128]{2,1,0:T(8,128)(2,1)}), bf16[16,16,128]{2,1,0:T(8,128)(2,1)S(1)}, u32[]{:S(2)}, u32[]{:S(2)}) async-start(bf16[16,16,128]{2,1,0:T(8,128)(2,1)} %get-tuple-element.8), calls=%async_computation.1 | async-start | bytes 131072 | tf_op jit(solution)/shard_map/all_to_all | solution.py:215
  172.7 10.2 %copy-start.2 = (bf16[2064,128]{1,0:T(8,128)(2,1)}, bf16[2064,128]{1,0:T(8,128)(2,1)S(1)}, u32[]{:S(2)}) copy-start(bf16[2064,128]{1,0:T(8,128)(2,1)S(1)} %broadcast_select_fusion.2.blocks_ref) | copy-start | bytes 1585156
  179.1 3.8 %copy-start.4 = (bf16[16,16,128]{2,1,0:T(8,128)(2,1)}, bf16[16,16,128]{2,1,0:T(8,128)(2,1)S(1)}, u32[]{:S(2)}) copy-start(bf16[16,16,128]{2,1,0:T(8,128)(2,1)S(1)} %all-to-all-done.1.mine_ref) | copy-start | bytes 196612
  179.1 3.8 %collective-permute-start.23 = (bf16[16,16,128]{2,1,0:T(8,128)(2,1)S(1)}, bf16[16,16,128]{2,1,0:T(8,128)(2,1)S(1)}, u32[]{:S(2)}, u32[]{:S(2)}) collective-permute-start(bf16[16,16,128]{2,1,0:T(8,128)(2,1)S(1)} %all-to-all-done.1.mine_ref), channel_id=1, source_target_pairs={{0,1},{1,0},{2,3},{3,2},{4,5},{5,4},{6,7},{7,6},{8,9},{9,8},{10,11... | collective-permute-start | bytes 196616 | tf_op jit(solution)/shard_map/ppermute | solution.py:26
  182.9 0.6 copy-start.6
  197.7 3.1 %collective-permute-start.24 = (f32[8,2,16,128]{3,2,1,0:T(8,128)S(1)}, f32[8,2,16,128]{3,2,1,0:T(8,128)S(1)}, u32[]{:S(2)}, u32[]{:S(2)}) collective-permute-start(f32[8,2,16,128]{3,2,1,0:T(8,128)S(1)} %all_to_all.15), channel_id=1, source_target_pairs={{0,1},{1,0},{2,3},{3,2},{4,5},{5,4},{6,7},{7,6},{8,9},{9,8},{10,11... | collective-permute-start | bytes 393224 | tf_op jit(solution)/shard_map/ppermute | solution.py:26

commit v2 on v1

v2 whole, which is shorter than its diff:
```python
import jax
import jax.numpy as jnp
from jax import lax
from jax.experimental import pallas as pl
from jax.experimental.pallas import tpu as pltpu
from jax.sharding import Mesh
from jax.sharding import PartitionSpec as P

F32 = jnp.float32
BF16 = jnp.bfloat16
Y, X, Z, C = 4, 4, 8, 2
STEPS, ROWS, SLOTS, BS = 8, 4, 8, 128
CH = 64
CHZ = CH // Z
SIDE = 2 * SLOTS * BS
PAIR = SIDE + 16
NT = (((1,), (1,)), ((), ()))
VMEM_LIMIT = 48 * 1024 * 1024
PACK_LIMIT = 58 * 1024 * 1024
SMALL_LIMIT = 4 * 1024 * 1024


def swap_cores(array):
    return lax.ppermute(array, "core", [(0, 1), (1, 0)])


def hop_pairs(phase, by):
    pairs = []
    for y in range(Y):
        for x in range(X):
            for z in range(Z):
                for core in range(C):
                    if core == phase:
                        to = (y, (x + by) % X)
                    else:
                        to = ((y + by) % Y, x)
                    pairs.append((((y * X + x) * Z + z) * C + core, ((to[0] * X + to[1]) * Z + z) * C + core))
    return pairs


def hop(array, phase, by):
    return lax.ppermute(array, ("y", "x", "z", "core"), hop_pairs(phase, by))


def near_hops(array, phase):
    return hop(array, phase, 1), hop(array, phase, -1)


def first_axis(history):
    below, above = near_hops(history, 0)
    half = STEPS // 2
    far = hop(below[:half], 0, 1), hop(above[half:], 0, -1)
    return jnp.concatenate([history, below]), jnp.concatenate([above, *far])


def entries(cols, steps):
    dy = (lax.axis_index("y") - cols // (X * ROWS)) % Y
    dx = (lax.axis_index("x") - (cols // ROWS) % X) % X
    dy, dx = dy ^ (dy >> 1), dx ^ (dx >> 1)
    slot = jnp.where(lax.axis_index("core") == 0, dy * X + dx, dx * Y + dy)
    return (slot * STEPS + steps) * ROWS + cols % ROWS


def pack_kernel(blocks_ref, pattern_ref, out_ref, codes, sems):
    copies = []
    for pair in range(2):
        for part in range(4):
            size = SIDE // 4
            source = blocks_ref.at[pl.ds(pair * SIDE + part * size, size)]
            target = out_ref.at[pair, pl.ds(part * size, size)]
            copies.append(pltpu.make_async_copy(source, target, sems.at[len(copies)]))
    for copy in copies:
        copy.start()
    codes[...] = jnp.zeros_like(codes)
    codes[:ROWS, :SLOTS] = pattern_ref[0].astype(F32)
    for pair in range(2):
        out_ref[pair, SIDE:] = codes[...].astype(BF16)
    for copy in copies:
        copy.wait()


def packed_front(blocks, pattern):
    return pl.pallas_call(
        pack_kernel,
        in_specs=[pl.BlockSpec(memory_space=pltpu.HBM), pl.BlockSpec(memory_space=pltpu.VMEM)],
        out_specs=pl.BlockSpec(memory_space=pltpu.VMEM),
        out_shape=jax.ShapeDtypeStruct((2, PAIR, BS), BF16),
        scratch_shapes=[pltpu.VMEM((16, BS), F32), pltpu.SemaphoreType.DMA((8,))],
        compiler_params=pltpu.CompilerParams(vmem_limit_bytes=PACK_LIMIT),
        name="packed_front",
    )(blocks.reshape(-1, BS), pattern)


def packed_codes(pack):
    return pack[SIDE : SIDE + ROWS, :SLOTS].astype(jnp.int32)


def picked_rows(table_ref, idx, base):
    parts = []
    for s in range(SLOTS):
        code = idx[base + s]
        lane = pl.multiple_of(lax.rem(code, ROWS) * BS, BS)
        parts.append(table_ref[lax.div(code, ROWS), :, pl.ds(lane, BS)])
    return jnp.concatenate(parts, axis=1)


def slot_product(rows, squares):
    return lax.dot_general(rows, jnp.concatenate(squares, axis=1), NT, preferred_element_type=F32)


def field_kernel(now_idx, past_idx, is_last, blocks_ref, next_ref, *refs):
    parts, (out_ref, acc, squares, table, sems) = refs[:PARTS], refs[PARTS:]
    size = parts[0].shape[0]
    tables = [
        pltpu.make_async_copy(part, table.at[pl.ds(i * size, size)], sems.at[STEPS + i]) for i, part in enumerate(parts)
    ]
    arriving = [pltpu.make_async_copy(blocks_ref.at[k], squares.at[k], sems.at[k]) for k in range(STEPS)]
    for copy in tables + arriving:
        copy.start()
    for copy in tables:
        copy.wait()
    for row in range(ROWS):
        last = picked_rows(table, past_idx, row * SLOTS)
        at = (row % 2) * SLOTS
        matrix = [next_ref[row // 2, (at + s) * BS : (at + s + 1) * BS] for s in range(SLOTS)]
        acc[row, CH:] = jnp.where(is_last[0] == 1, 0.0, slot_product(last, matrix))
    for k in range(STEPS):
        arriving[k].wait()
        for row in range(ROWS):
            base = (k * ROWS + row) * SLOTS
            matrix = [squares[k, row, s] for s in range(SLOTS)]
            now = picked_rows(table, now_idx, base)
            if k == 0:
                acc[row, :CH] = slot_product(now, matrix)
            else:
                past = picked_rows(table, past_idx, base)
                acc[row] += slot_product(jnp.concatenate([now, past]), matrix)
    for row in range(ROWS):
        for f in range(2):
            for z in range(Z):
                start = f * CH + z * CHZ
                out_ref[z, row // 2, row % 2, f] = acc[row, start : start + CHZ]


IN_SMEM = pl.BlockSpec(memory_space=pltpu.SMEM)
IN_VMEM = pl.BlockSpec(memory_space=pltpu.VMEM)
IN_HBM = pl.BlockSpec(memory_space=pltpu.HBM)
ANYWHERE = pl.BlockSpec(memory_space=pl.ANY)
SLAB = (CH, ROWS * BS)
PARTS = 8


def field_partials(blocks, following, parts, now_idx, past_idx, is_last):
    return pl.pallas_call(
        field_kernel,
        in_specs=[IN_SMEM] * 3 + [IN_HBM, IN_VMEM] + [ANYWHERE] * PARTS,
        out_specs=IN_VMEM,
        out_shape=jax.ShapeDtypeStruct((Z, C, 2, 2, CHZ, BS), F32),
        scratch_shapes=[
            pltpu.VMEM((ROWS, 2 * CH, BS), F32),
            pltpu.VMEM((STEPS, ROWS, SLOTS, BS, BS), BF16),
            pltpu.VMEM((Y * X * STEPS, *SLAB), BF16),
            pltpu.SemaphoreType.DMA((STEPS + PARTS,)),
        ],
        compiler_params=pltpu.CompilerParams(vmem_limit_bytes=VMEM_LIMIT),
        cost_estimate=pl.CostEstimate(flops=1 << 30, bytes_accessed=1 << 24, transcendentals=0),
        name="field_partials",
    )(now_idx, past_idx, is_last, blocks, following, *parts)


def exact_dot(a, b):
    return lax.dot_general(a, b, NT, precision=lax.Precision.HIGHEST, preferred_element_type=F32)


def first_kernel(parts_ref, excite_ref, near_ref, current_ref, low_ref, rest_ref):
    total = parts_ref[0]
    for band in range(1, Z * C):
        total = total + parts_ref[band]
    solved = []
    for row in range(2):
        at = row * 2 * CHZ
        field = excite_ref[0, row] - total[at : at + CHZ]
        solved.append(exact_dot(field, near_ref[row]))
        rest_ref[row] = excite_ref[1, row] - total[at + CHZ : at + 2 * CHZ]
    both = jnp.concatenate(solved, axis=0)
    current_ref[...] = both
    low = both.astype(BF16)
    for s in range(Y * X):
        low_ref[s] = low


def first_solve(parts, excite, near):
    return pl.pallas_call(
        first_kernel,
        out_shape=(
            jax.ShapeDtypeStruct((2 * CHZ, BS), F32),
            jax.ShapeDtypeStruct((Y * X, 2 * CHZ, BS), BF16),
            jax.ShapeDtypeStruct((2, CHZ, BS), F32),
        ),
        compiler_params=pltpu.CompilerParams(vmem_limit_bytes=SMALL_LIMIT),
        name="first_solve",
    )(parts, excite, near)


def second_kernel(idx, mine_ref, other_ref, blocks_ref, rest_ref, near_ref, current_ref, out_ref, table):
    for h, ref in enumerate((mine_ref, other_ref)):
        for s in range(Y * X):
            wide = ref[s].astype(F32)
            for row in range(2):
                table[(h * Y * X + s) * 2 + row] = wide[row * CHZ : (row + 1) * CHZ]
    solved = []
    for row in range(2):
        picked = [table[idx[row * SLOTS + s]].astype(BF16) for s in range(SLOTS)]
        matrix = jnp.concatenate([blocks_ref[(row * SLOTS + s) * BS : (row * SLOTS + s + 1) * BS] for s in range(SLOTS)], axis=1)
        term = lax.dot_general(jnp.concatenate(picked, axis=1), matrix, NT, preferred_element_type=F32)
        solved.append(exact_dot(rest_ref[row] - term, near_ref[row]))
    second = jnp.concatenate(solved, axis=0)
    first = current_ref[...]
    for z in range(Z):
        out_ref[z, 0] = first
        out_ref[z, 1] = second


def second_solve(idx, mine, other, blocks, rest, near, current):
    return pl.pallas_call(
        second_kernel,
        in_specs=[pl.BlockSpec(memory_space=pltpu.SMEM)] + [pl.BlockSpec(memory_space=pltpu.VMEM)] * 6,
        out_specs=pl.BlockSpec(memory_space=pltpu.VMEM),
        out_shape=jax.ShapeDtypeStruct((Z, 2, 2 * CHZ, BS), F32),
        scratch_shapes=[pltpu.VMEM((2 * Y * X * 2, CHZ, BS), F32)],
        compiler_params=pltpu.CompilerParams(vmem_limit_bytes=SMALL_LIMIT),
        name="second_solve",
    )(idx, mine, other, blocks, rest, near, current)


SPREAD = (((0, 2), (7, 5)), ((0, 1), (2, 3), (5, 4), (7, 6)))


def spread(array, step, tie):
    z = lax.axis_index("z")
    received = lax.ppermute(tie(array), "z", SPREAD[step])
    hit = z == SPREAD[step][0][1]
    for _, target in SPREAD[step][1:]:
        hit = hit | (z == target)
    return jnp.where(hit, received, array)


def after(array, *events):
    return lax.optimization_barrier((array, *events))[0]


def local(excitation, history, blocks, pattern, near_inverse):
    core, z = lax.axis_index("core"), lax.axis_index("z")
    bands = lax.axis_size(("z", "core"))

    line = first_axis(history)
    pack = packed_front(blocks, pattern)
    below = hop(line[0], 1, 1)
    above = hop(line[1], 1, -1)
    below_rest = hop(line[1], 1, 1)
    above_rest = hop(line[0], 1, -1)
    far = hop(below, 1, 1), hop(above, 1, -1)
    following = lax.ppermute(pack, ("z", "core"), [(i, (i - 1) % bands) for i in range(bands)])
    given = jnp.where(core == 0, pack[1], following[0])
    front = jnp.where(z == 0, pack[0], following[1])
    front = jnp.where(core == (z == 0), swap_cores(given), front)
    front = spread(front, 0, lambda new: after(new, below_rest, above_rest))

    pattern = after(pattern, line)
    steps = jnp.arange(STEPS, dtype=jnp.int32)[:, None, None]
    now_idx = entries(pattern, steps)
    past_cols = jnp.concatenate([packed_codes(following[0])[None], pattern[1:]])
    past_idx = entries(past_cols, (steps - 1) % STEPS)
    parts = (*line, below, below_rest, above_rest, above, *far)
    is_last = (z * C + core == bands - 1).astype(jnp.int32).reshape(1)
    partial = field_partials(blocks, following, parts, now_idx.reshape(-1), past_idx.reshape(-1), is_last)
    parts = lax.all_to_all(partial.reshape(Z * C, 4 * CHZ, BS), ("z", "core"), 0, 0)

    excite = lax.dynamic_slice(excitation, (0, z * CHZ, core * 2 * BS), (2, CHZ, 2 * BS))
    excite = excite.reshape(2, CHZ, 2, BS).transpose(0, 2, 1, 3)
    near = lax.dynamic_slice(near_inverse, (core * 2, 0, 0), (2, BS, BS))
    current, low, rest = first_solve(parts, excite, near)
    front = spread(front, 1, lambda new: after(new, current))

    mine = lax.all_to_all(low, ("y", "x"), 0, 0)
    other = swap_cores(mine)
    front_cols = lax.dynamic_slice_in_dim(packed_codes(front), core * 2, 2).reshape(-1)
    front_idx = (((front_cols % ROWS) // 2 ^ core) * Y * X + front_cols // ROWS) * 2 + front_cols % 2
    ready = second_solve(front_idx, mine, other, front, rest, near, current)

    kept = lax.all_to_all(ready, "z", 0, 0)
    given = swap_cores(kept)
    both = jnp.stack([jnp.where(core == 0, kept, given), jnp.where(core == 0, given, kept)])
    both = both.reshape(C, Z, 2, 2, CHZ, BS)
    return both.transpose(2, 1, 4, 0, 3, 5).reshape(2, CH, ROWS * BS)


def solution(mesh):
    split = Mesh(mesh.devices.reshape(Y, X, Z, C), ("y", "x", "z", "core"))
    surf, hist = ("y", "x"), ("z", "core")
    in_specs = (
        P(None, None, surf),
        P(hist, None, surf),
        P(hist, surf, None, None, None),
        P(hist, surf, None),
        P(surf, None, None),
    )
    out_specs = P(None, None, surf)
    return jax.shard_map(local, mesh=split, in_specs=in_specs, out_specs=out_specs, check_vma=False)
```

time: 203 us -> 123 us (0.61)
  waiting for transfers between devices: 66.5 us -> 29.3 us
  local copies, waits for them, and re-layouts: 41.1 us -> 9.61 us
  starting transfers between devices: 58.9 us -> 51.8 us
  Pallas kernels: 16.9 us -> 13.3 us
    ppermute x22 -> x13, waiting for transfers between devices: 49.8 us -> 10.5 us  [the longest x10 10.5 us: hop(): return lax.ppermute(array, ('y', 'x', 'z', 'core'), hop_pairs(phase, by))]
    unnamed x29 -> x15, local copies, waits for them, and re-layouts: 20.7 us -> 2.72 us
    ppermute x22 -> x13, starting transfers between devices: 39.5 us -> 26.2 us  [the longest x10 16.6 us: hop(): return lax.ppermute(array, ('y', 'x', 'z', 'core'), hop_pairs(phase, by))]
    gather x6 -> x0, local copies, waits for them, and re-layouts: 5.32 us -> none  [the longest x3 2.66 us: entries(): dy = place[(lax.axis_index('y') - cols // (X * ROWS)) % Y]]
    ppermute x3, starting transfers between devices: 6.97 us -> 10.8 us  [swap_cores(): return lax.ppermute(array, 'core', [(0, 1), (1, 0)])]
    squeeze x3 -> x1, local copies, waits for them, and re-layouts: 4.37 us -> 1.08 us  [local(): given = jnp.where(core == 0, pack[1], following[0])]
    slice x10 -> x4, local copies, waits for them, and re-layouts: 3.82 us -> 0.75 us  [the longest x2 0.74 us: first_axis(): far = (hop(below[:half], 0, 1), hop(above[half:], 0, -1))]
    select_n x6 -> x5, other arithmetic: 2.96 us -> 4.47 us  [the longest x1 1.94 us: local(): front = jnp.where(core == (z == 0), swap_cores(given), front)]
  transfers between devices with their start and end apart: 27 -> 18, of which waited for: 9 -> 7; matrix products, arithmetic and copies ran while one was open for 21% -> 12% of each run, Pallas kernels for 7% -> 9%
where the time goes in v2:
time: 123 us; the launch traced here: 122 us
  starting transfers between devices  51.8 us (42%)
  waiting for transfers between devices  29.3 us (24%)
  Pallas kernels  13.3 us (11%)
  blocking collectives  10.9 us (9%)
  local copies, waits for them, and re-layouts  9.61 us (8%)
  other arithmetic  6.59 us (5%)
    ppermute x10, starting transfers between devices, hop(): return lax.ppermute(array, ('y', 'x', 'z', 'core'), hop_pairs(phase, by))  16.6 us
    all_to_all x1, blocking collectives, local(): kept = lax.all_to_all(ready, 'z', 0, 0)  10.9 us
    ppermute x3, starting transfers between devices, swap_cores(): return lax.ppermute(array, 'core', [(0, 1), (1, 0)])  10.8 us
    all_to_all x1, waiting for transfers between devices, local(): lax.all_to_all(partial.reshape(Z * C, 4 * CHZ, BS), ('z', 'core'), 0, 0)  10.6 us
    ppermute x10, waiting for transfers between devices, hop(): return lax.ppermute(array, ('y', 'x', 'z', 'core'), hop_pairs(phase, by))  10.5 us
    all_to_all x1, starting transfers between devices, local(): lax.all_to_all(partial.reshape(Z * C, 4 * CHZ, BS), ('z', 'core'), 0, 0)  9.85 us
    pallas_call x1, Pallas kernels, field_partials(): pl.pallas_call(field_kernel, in_specs=[IN_SMEM] * 3 + [IN_HBM, IN_VMEM] +...  8 us
    ppermute x2, starting transfers between devices, spread(): received = lax.ppermute(tie(array), 'z', SPREAD[step])  6.73 us
  transfers between devices with their start and end apart: 18, of which 7 were waited for; matrix products, arithmetic and copies ran while one was open for 12% of the time, Pallas kernels for 9%

profile of v2, /device:TPU:1, one launch (start us, length us, event | category | flops | bytes accessed | tf_op | source)
XLA Modules:
  0.0 121.8 jit_solution(17337677017215593828)
XLA Ops:
  0.0 2.1 %collective-permute-start.3 = (bf16[8,64,512]{2,1,0:T(8,128)(2,1)}, bf16[8,64,512]{2,1,0:T(8,128)(2,1)S(1)}, u32[]{:S(2)}, u32[]{:S(2)}) collective-permute-start(bf16[8,64,512]{2,1,0:T(8,128)(2,1)} %param.6), channel_id=1, source_target_pairs={{0,16},{1,65},{2,18},{3,67},{4,20},{5,69},{6,22},{7,71},{8,24},{9,... | collective-permute-start | bytes 1572872 | tf_op jit(solution)/shard_map/ppermute | solution.py:42
  2.1 1.5 %collective-permute-start.2 = (bf16[8,64,512]{2,1,0:T(8,128)(2,1)}, bf16[8,64,512]{2,1,0:T(8,128)(2,1)S(1)}, u32[]{:S(2)}, u32[]{:S(2)}) collective-permute-start(bf16[8,64,512]{2,1,0:T(8,128)(2,1)} %param.6), channel_id=1, source_target_pairs={{0,48},{1,193},{2,50},{3,195},{4,52},{5,197},{6,54},{7,199},{8,56}... | collective-permute-start | bytes 1572872 | tf_op jit(solution)/shard_map/ppermute | solution.py:42
  3.7 3.1 %packed_front.1 = bf16[2,2064,128]{2,1,0:T(8,128)(2,1)} custom-call(bf16[32768,128]{1,0:T(8,128)(2,1)} %bitcast.31, s32[8,4,8]{2,1,0:T(4,128)} %pattern_ref.1), custom_call_target="tpu_custom_call" | custom-call | tf_op jit(solution)/shard_map/packed_front/pallas_call | solution.py:83
  6.8 2.8 %collective-permute-start = (bf16[2,2064,128]{2,1,0:T(8,128)(2,1)}, bf16[2,2064,128]{2,1,0:T(8,128)(2,1)}, u32[]{:S(2)}, u32[]{:S(2)}) collective-permute-start(bf16[2,2064,128]{2,1,0:T(8,128)(2,1)} %packed_front.1), channel_id=1, source_target_pairs={{0,15},{1,0},{2,1},{3,2},{4,3},{5,4},{6,5},{7,6},{8,7},{9,8},{10,9... | collective-permute-start | bytes 3170312 | tf_op jit(solution)/shard_map/ppermute | solution.py:263
  9.6 0.7 dynamic-slice_bitcast_fusion.excite_ref
  10.4 0.3 collective-permute-done.3
  10.6 0.7 slice.41
  11.4 0.0 collective-permute-start.4
  11.4 0.1 add.147
  11.5 0.6 add.148
  12.1 2.7 %collective-permute-start.5 = (bf16[4,64,512]{2,1,0:T(8,128)(2,1)S(1)}, bf16[4,64,512]{2,1,0:T(8,128)(2,1)S(1)}, u32[]{:S(2)}, u32[]{:S(2)}) collective-permute-start(bf16[4,64,512]{2,1,0:T(8,128)(2,1)S(1)} %slice.42), channel_id=1, source_target_pairs={{0,48},{1,193},{2,50},{3,195},{4,52},{5,197},{6,54},{7,199},{8,56}... | collective-permute-start | bytes 786440 | tf_op jit(solution)/shard_map/ppermute | solution.py:42
  14.9 2.6 %collective-permute-start.7 = (bf16[16,64,512]{2,1,0:T(8,128)(2,1)S(1)}, bf16[16,64,512]{2,1,0:T(8,128)(2,1)S(1)}, u32[]{:S(2)}, u32[]{:S(2)}) collective-permute-start(bf16[16,64,512]{2,1,0:T(8,128)(2,1)S(1)} %constant_dynamic-update-slice_fusion.3.refs_0_), channel_id=1, source_target_pairs={{0,192},{1,49},{2,194},{3,51},{4,196},{5,53},{6,198},{7,55},{8,200... | collective-permute-start | bytes 3145736 | tf_op jit(solution)/shard_map/ppermute | solution.py:42
  17.5 1.1 constant_dynamic-update-slice_fusion.2
  18.6 1.0 constant_dynamic-update-slice_fusion.1
  19.6 0.5 collective-permute-start.6
  20.1 2.3 %collective-permute-start.10 = (bf16[16,64,512]{2,1,0:T(8,128)(2,1)S(1)}, bf16[16,64,512]{2,1,0:T(8,128)(2,1)}, u32[]{:S(2)}, u32[]{:S(2)}) collective-permute-start(bf16[16,64,512]{2,1,0:T(8,128)(2,1)S(1)} %constant_dynamic-update-slice_fusion.refs_1_), channel_id=1, source_target_pairs={{0,192},{1,49},{2,194},{3,51},{4,196},{5,53},{6,198},{7,55},{8,200... | collective-permute-start | bytes 3145736 | tf_op jit(solution)/shard_map/ppermute | solution.py:42
  22.4 0.7 fusion.9
  23.1 1.3 %reshape.56.now_idx = s32[256]{0:T(256)} reshape(s32[8,4,8]{2,1,0:T(4,128)} %fusion.9) | data formatting | bytes 2048 | tf_op jit(solution)/shard_map/reshape | solution.py:276
  24.5 1.3 %fusion.2 = bf16[2064,128]{1,0:T(8,128)(2,1)S(1)} fusion(bf16[2,2064,128]{2,1,0:T(8,128)(2,1)} %packed_front.1, pred[]{:T(512)S(6)} %eq.49, bf16[2,2064,128]{2,1,0:T(8,128)(2,1)} %collective-permute-done.next_ref), kind=kLoop, calls=%fused_computation.5 | loop fusion | flops 264192 | bytes 1585153 | tf_op jit(solution)/shard_map/jit(_where)/select_n | solution.py:264
  25.8 6.8 %collective-permute-start.1 = (bf16[2064,128]{1,0:T(8,128)(2,1)S(1)}, bf16[2064,128]{1,0:T(8,128)(2,1)S(1)}, u32[]{:S(2)}, u32[]{:S(2)}) collective-permute-start(bf16[2064,128]{1,0:T(8,128)(2,1)S(1)} %fusion.2), channel_id=1, source_target_pairs={{0,1},{1,0},{2,3},{3,2},{4,5},{5,4},{6,7},{7,6},{8,9},{9,8},{10,11... | collective-permute-start | bytes 1585160 | tf_op jit(solution)/shard_map/ppermute | solution.py:24
  32.6 1.1 slice_bitcast_fusion
  33.7 1.3 %collective-permute-start.11 = (bf16[16,64,512]{2,1,0:T(8,128)(2,1)}, bf16[16,64,512]{2,1,0:T(8,128)(2,1)}, u32[]{:S(2)}, u32[]{:S(2)}) collective-permute-start(bf16[16,64,512]{2,1,0:T(8,128)(2,1)} %collective-permute-done.9.refs_2_), channel_id=1, source_target_pairs={{0,64},{1,17},{2,66},{3,19},{4,68},{5,21},{6,70},{7,23},{8,72},{9,... | collective-permute-start | bytes 3145736 | tf_op jit(solution)/shard_map/ppermute | solution.py:42
  35.0 8.2 %collective-permute-done.10.refs_5_ = bf16[16,64,512]{2,1,0:T(8,128)(2,1)} collective-permute-done((bf16[16,64,512]{2,1,0:T(8,128)(2,1)S(1)}, bf16[16,64,512]{2,1,0:T(8,128)(2,1)}, u32[]{:S(2)}, u32[]{:S(2)}) %collective-permute-start.10) | collective-permute-done | bytes 1048608 | tf_op jit(solution)/shard_map/ppermute | solution.py:42
  43.3 3.5 %collective-permute-start.12 = (bf16[16,64,512]{2,1,0:T(8,128)(2,1)}, bf16[16,64,512]{2,1,0:T(8,128)(2,1)}, u32[]{:S(2)}, u32[]{:S(2)}) collective-permute-start(bf16[16,64,512]{2,1,0:T(8,128)(2,1)} %collective-permute-done.10.refs_5_), channel_id=1, source_target_pairs={{0,192},{1,49},{2,194},{3,51},{4,196},{5,53},{6,198},{7,55},{8,200... | collective-permute-start | bytes 3145736 | tf_op jit(solution)/shard_map/ppermute | solution.py:42
  46.8 1.9 %fusion.1 = bf16[2064,128]{1,0:T(8,128)(2,1)} fusion(bf16[2064,128]{1,0:T(8,128)(2,1)S(1)} %collective-permute-done.1, bf16[2,2064,128]{2,1,0:T(8,128)(2,1)} %collective-permute-done.next_ref, bf16[2,2064,128]{2,1,0:T(8,128)(2,1)S(1)} %copy-done.2, pred[]{:T(512)S(6)} %eq.56, pred[]{:T(512)S(6)} %eq.57), kind=kLoop, calls=%fused_computation.2 | loop fusion | flops 528384 | bytes 2113538 | tf_op jit(solution)/shard_map/jit(_where)/select_n | solution.py:266
  48.7 5.3 %collective-permute-start.8 = (bf16[2064,128]{1,0:T(8,128)(2,1)}, bf16[2064,128]{1,0:T(8,128)(2,1)}, u32[]{:S(2)}, u32[]{:S(2)}) collective-permute-start(bf16[2064,128]{1,0:T(8,128)(2,1)} %fusion.1), channel_id=1, source_target_pairs={{0,4},{14,10},{1,5},{15,11},{16,20},{30,26},{17,21},{31,27},{32,36... | collective-permute-start | bytes 1585160 | tf_op jit(solution)/shard_map/ppermute | solution.py:241
  54.0 0.6 pad_add_fusion
  54.6 1.4 %concatenate.15 = s32[256]{0:T(256)} reshape(s32[8,4,8]{2,1,0:T(4,128)} %pad_add_fusion) | data formatting | bytes 2048 | tf_op jit(solution)/shard_map/concatenate | solution.py:272
  56.1 0.7 fusion.11.past_idx
  56.8 2.0 %collective-permute-done.12.refs_7_ = bf16[16,64,512]{2,1,0:T(8,128)(2,1)} collective-permute-done((bf16[16,64,512]{2,1,0:T(8,128)(2,1)}, bf16[16,64,512]{2,1,0:T(8,128)(2,1)}, u32[]{:S(2)}, u32[]{:S(2)}) %collective-permute-start.12) | collective-permute-done | bytes 1048608 | tf_op jit(solution)/shard_map/ppermute | solution.py:42
  58.8 0.6 copy-done.1
  59.5 8.0 %field_partials.1 = f32[8,2,2,2,8,128]{5,4,3,2,1,0:T(8,128)} custom-call(s32[256]{0:T(256)S(1)} %copy-done.1, s32[256]{0:T(256)S(1)} %fusion.11.past_idx, s32[1]{0:T(128)} %bitcast.5.is_last, bf16[8,4,8,128,128]{4,3,2,1,0:T(8,128)(2,1)} %blocks_ref.1, bf16[2,2064,128]{2,1,0:T(8,128)(2,1)} %collective-permute-done.next_ref, ...), custom_call_target="tpu_custom_call" | custom-call | flops 1073741824 | bytes 16777216 | tf_op jit(solution)/shard_map/field_partials/pallas_call | solution.py:154
  67.5 9.9 %all-to-all-start = ((f32[16,32,128]{2,1,0:T(8,128)}), f32[16,32,128]{2,1,0:T(8,128)S(1)}, u32[]{:S(2)}, u32[]{:S(2)}) async-start(f32[16,32,128]{2,1,0:T(8,128)} %bitcast.6), calls=%async_computation | async-start | bytes 524288 | tf_op jit(solution)/shard_map/all_to_all | solution.py:277
  77.3 1.1 broadcast_select_fusion
  78.4 10.6 %all-to-all-done.parts_ref = f32[16,32,128]{2,1,0:T(8,128)S(1)} async-done(((f32[16,32,128]{2,1,0:T(8,128)}), f32[16,32,128]{2,1,0:T(8,128)S(1)}, u32[]{:S(2)}, u32[]{:S(2)}) %all-to-all-start) | async-done | bytes 262176 | tf_op jit(solution)/shard_map/all_to_all | solution.py:277
  89.0 1.0 first_solve.1
  90.0 1.4 %collective-permute-start.13 = (bf16[2064,128]{1,0:T(8,128)(2,1)S(1)}, bf16[2064,128]{1,0:T(8,128)(2,1)S(1)}, u32[]{:S(2)}, u32[]{:S(2)}) collective-permute-start(bf16[2064,128]{1,0:T(8,128)(2,1)S(1)} %broadcast_select_fusion), channel_id=1, source_target_pairs={{0,2},{4,6},{10,8},{14,12},{1,3},{5,7},{11,9},{15,13},{16,18},{20,... | collective-permute-start | bytes 1585160 | tf_op jit(solution)/shard_map/ppermute | solution.py:241
  91.4 5.0 %all-to-all-start.1 = ((bf16[16,16,128]{2,1,0:T(8,128)(2,1)}), bf16[16,16,128]{2,1,0:T(8,128)(2,1)S(1)}, u32[]{:S(2)}, u32[]{:S(2)}) async-start(bf16[16,16,128]{2,1,0:T(8,128)(2,1)} %get-tuple-element.15), calls=%async_computation.1 | async-start | bytes 131072 | tf_op jit(solution)/shard_map/all_to_all | solution.py:285
  96.4 6.5 %all-to-all-done.1.mine_ref = bf16[16,16,128]{2,1,0:T(8,128)(2,1)S(1)} async-done(((bf16[16,16,128]{2,1,0:T(8,128)(2,1)}), bf16[16,16,128]{2,1,0:T(8,128)(2,1)S(1)}, u32[]{:S(2)}, u32[]{:S(2)}) %all-to-all-start.1) | async-done | bytes 65568 | tf_op jit(solution)/shard_map/all_to_all | solution.py:285
  102.9 1.9 %collective-permute-start.14 = (bf16[16,16,128]{2,1,0:T(8,128)(2,1)S(1)}, bf16[16,16,128]{2,1,0:T(8,128)(2,1)S(1)}, u32[]{:S(2)}, u32[]{:S(2)}) collective-permute-start(bf16[16,16,128]{2,1,0:T(8,128)(2,1)S(1)} %all-to-all-done.1.mine_ref), channel_id=1, source_target_pairs={{0,1},{1,0},{2,3},{3,2},{4,5},{5,4},{6,7},{7,6},{8,9},{9,8},{10,11... | collective-permute-start | bytes 196616 | tf_op jit(solution)/shard_map/ppermute | solution.py:24
  104.8 0.1 broadcast_select_fusion.1.blocks_ref
  104.9 0.1 reshape.61
  105.0 0.7 collective-permute-done.14.other_ref
  105.7 1.3 %second_solve.1 = f32[8,2,16,128]{3,2,1,0:T(8,128)S(1)} custom-call(s32[16]{0:T(128)S(1)} %fusion.16.idx, bf16[16,16,128]{2,1,0:T(8,128)(2,1)S(1)} %all-to-all-done.1.mine_ref, bf16[16,16,128]{2,1,0:T(8,128)(2,1)S(1)} %collective-permute-done.14.other_ref, bf16[2064,128]{1,0:T(8,128)(2,1)S(1)} %broadcast_select_fusion.1.blocks_ref, ...), custom_call_target="tpu_custom_call" | custom-call | tf_op jit(solution)/shard_map/second_solve/pallas_call | solution.py:225
  107.0 10.9 %all_to_all.15 = f32[8,2,16,128]{3,2,1,0:T(8,128)S(1)} all-to-all(f32[8,2,16,128]{3,2,1,0:T(8,128)S(1)} %second_solve.1), channel_id=1, replica_groups=mesh['y'=4,'x'=4,'z'=8,'core'=2] {'z'}, dimensions={0} | all-to-all | bytes 262144 | tf_op jit(solution)/shard_map/all_to_all | solution.py:291
  117.9 2.1 %collective-permute-start.15 = (f32[8,2,16,128]{3,2,1,0:T(8,128)S(1)}, f32[8,2,16,128]{3,2,1,0:T(8,128)S(1)}, u32[]{:S(2)}, u32[]{:S(2)}) collective-permute-start(f32[8,2,16,128]{3,2,1,0:T(8,128)S(1)} %all_to_all.15), channel_id=1, source_target_pairs={{0,1},{1,0},{2,3},{3,2},{4,5},{5,4},{6,7},{7,6},{8,9},{9,8},{10,11... | collective-permute-start | bytes 393224 | tf_op jit(solution)/shard_map/ppermute | solution.py:24
  120.0 1.0 collective-permute-done.15
  121.0 0.7 copy.6
  (37 shorter events, 0.3 us)
Async XLA Ops:
  0.0 9.6 %copy-start = (f32[4,128,128]{2,1,0:T(8,128)S(1)}, f32[4,128,128]{2,1,0:T(8,128)}, u32[]{:S(2)}) copy-start(f32[4,128,128]{2,1,0:T(8,128)} %param.9) | copy-start | bytes 786436
  0.0 10.6 %collective-permute-start.3 = (bf16[8,64,512]{2,1,0:T(8,128)(2,1)}, bf16[8,64,512]{2,1,0:T(8,128)(2,1)S(1)}, u32[]{:S(2)}, u32[]{:S(2)}) collective-permute-start(bf16[8,64,512]{2,1,0:T(8,128)(2,1)} %param.6), channel_id=1, source_target_pairs={{0,16},{1,65},{2,18},{3,67},{4,20},{5,69},{6,22},{7,71},{8,24},{9,... | collective-permute-start | bytes 1572872 | tf_op jit(solution)/shard_map/ppermute | solution.py:42
  2.1 10.0 %collective-permute-start.2 = (bf16[8,64,512]{2,1,0:T(8,128)(2,1)}, bf16[8,64,512]{2,1,0:T(8,128)(2,1)S(1)}, u32[]{:S(2)}, u32[]{:S(2)}) collective-permute-start(bf16[8,64,512]{2,1,0:T(8,128)(2,1)} %param.6), channel_id=1, source_target_pairs={{0,48},{1,193},{2,50},{3,195},{4,52},{5,197},{6,54},{7,199},{8,56}... | collective-permute-start | bytes 1572872 | tf_op jit(solution)/shard_map/ppermute | solution.py:42
  3.7 6.7 %copy-start.4 = (bf16[8,64,512]{2,1,0:T(8,128)(2,1)S(1)}, bf16[8,64,512]{2,1,0:T(8,128)(2,1)}, u32[]{:S(2)}) copy-start(bf16[8,64,512]{2,1,0:T(8,128)(2,1)} %param.6) | copy-start | bytes 1572868
  6.8 17.7 %collective-permute-start = (bf16[2,2064,128]{2,1,0:T(8,128)(2,1)}, bf16[2,2064,128]{2,1,0:T(8,128)(2,1)}, u32[]{:S(2)}, u32[]{:S(2)}) collective-permute-start(bf16[2,2064,128]{2,1,0:T(8,128)(2,1)} %packed_front.1), channel_id=1, source_target_pairs={{0,15},{1,0},{2,1},{3,2},{4,3},{5,4},{6,5},{7,6},{8,7},{9,8},{10,9... | collective-permute-start | bytes 3170312 | tf_op jit(solution)/shard_map/ppermute | solution.py:263
  11.4 7.2 %collective-permute-start.4 = (bf16[4,64,512]{2,1,0:T(8,128)(2,1)}, bf16[4,64,512]{2,1,0:T(8,128)(2,1)}, u32[]{:S(2)}, u32[]{:S(2)}) collective-permute-start(bf16[4,64,512]{2,1,0:T(8,128)(2,1)} %slice.41), channel_id=1, source_target_pairs={{0,16},{1,65},{2,18},{3,67},{4,20},{5,69},{6,22},{7,71},{8,24},{9,... | collective-permute-start | bytes 786440 | tf_op jit(solution)/shard_map/ppermute | solution.py:42
  12.1 2.8 %copy-start.3 = (bf16[8,64,512]{2,1,0:T(8,128)(2,1)}, bf16[8,64,512]{2,1,0:T(8,128)(2,1)S(1)}, u32[]{:S(2)}) copy-start(bf16[8,64,512]{2,1,0:T(8,128)(2,1)S(1)} %collective-permute-done.2) | copy-start | bytes 1572868
  12.1 7.4 %collective-permute-start.5 = (bf16[4,64,512]{2,1,0:T(8,128)(2,1)S(1)}, bf16[4,64,512]{2,1,0:T(8,128)(2,1)S(1)}, u32[]{:S(2)}, u32[]{:S(2)}) collective-permute-start(bf16[4,64,512]{2,1,0:T(8,128)(2,1)S(1)} %slice.42), channel_id=1, source_target_pairs={{0,48},{1,193},{2,50},{3,195},{4,52},{5,197},{6,54},{7,199},{8,56}... | collective-permute-start | bytes 786440 | tf_op jit(solution)/shard_map/ppermute | solution.py:42
  14.9 7.5 %copy-start.5 = (s32[8,4,8]{2,1,0:T(4,128)S(1)}, s32[8,4,8]{2,1,0:T(4,128)}, u32[]{:S(2)}) copy-start(s32[8,4,8]{2,1,0:T(4,128)} %pattern_ref.1) | copy-start | bytes 3076
  14.9 33.8 %collective-permute-start.7 = (bf16[16,64,512]{2,1,0:T(8,128)(2,1)S(1)}, bf16[16,64,512]{2,1,0:T(8,128)(2,1)S(1)}, u32[]{:S(2)}, u32[]{:S(2)}) collective-permute-start(bf16[16,64,512]{2,1,0:T(8,128)(2,1)S(1)} %constant_dynamic-update-slice_fusion.3.refs_0_), channel_id=1, source_target_pairs={{0,192},{1,49},{2,194},{3,51},{4,196},{5,53},{6,198},{7,55},{8,200... | collective-permute-start | bytes 3145736 | tf_op jit(solution)/shard_map/ppermute | solution.py:42
  17.5 16.3 %collective-permute-start.9 = (bf16[16,64,512]{2,1,0:T(8,128)(2,1)S(1)}, bf16[16,64,512]{2,1,0:T(8,128)(2,1)}, u32[]{:S(2)}, u32[]{:S(2)}) collective-permute-start(bf16[16,64,512]{2,1,0:T(8,128)(2,1)S(1)} %constant_dynamic-update-slice_fusion.3.refs_0_), channel_id=1, source_target_pairs={{0,64},{1,17},{2,66},{3,19},{4,68},{5,21},{6,70},{7,23},{8,72},{9,... | collective-permute-start | bytes 3145736 | tf_op jit(solution)/shard_map/ppermute | solution.py:42
  19.6 29.1 %collective-permute-start.6 = (bf16[16,64,512]{2,1,0:T(8,128)(2,1)S(1)}, bf16[16,64,512]{2,1,0:T(8,128)(2,1)}, u32[]{:S(2)}, u32[]{:S(2)}) collective-permute-start(bf16[16,64,512]{2,1,0:T(8,128)(2,1)S(1)} %constant_dynamic-update-slice_fusion.refs_1_), channel_id=1, source_target_pairs={{0,64},{1,17},{2,66},{3,19},{4,68},{5,21},{6,70},{7,23},{8,72},{9,... | collective-permute-start | bytes 3145736 | tf_op jit(solution)/shard_map/ppermute | solution.py:42
  20.1 23.1 %collective-permute-start.10 = (bf16[16,64,512]{2,1,0:T(8,128)(2,1)S(1)}, bf16[16,64,512]{2,1,0:T(8,128)(2,1)}, u32[]{:S(2)}, u32[]{:S(2)}) collective-permute-start(bf16[16,64,512]{2,1,0:T(8,128)(2,1)S(1)} %constant_dynamic-update-slice_fusion.refs_1_), channel_id=1, source_target_pairs={{0,192},{1,49},{2,194},{3,51},{4,196},{5,53},{6,198},{7,55},{8,200... | collective-permute-start | bytes 3145736 | tf_op jit(solution)/shard_map/ppermute | solution.py:42
  24.5 22.3 %copy-start.2 = (bf16[2,2064,128]{2,1,0:T(8,128)(2,1)S(1)}, bf16[2,2064,128]{2,1,0:T(8,128)(2,1)}, u32[]{:S(2)}) copy-start(bf16[2,2064,128]{2,1,0:T(8,128)(2,1)} %packed_front.1) | copy-start | bytes 3170308
  25.8 20.9 %collective-permute-start.1 = (bf16[2064,128]{1,0:T(8,128)(2,1)S(1)}, bf16[2064,128]{1,0:T(8,128)(2,1)S(1)}, u32[]{:S(2)}, u32[]{:S(2)}) collective-permute-start(bf16[2064,128]{1,0:T(8,128)(2,1)S(1)} %fusion.2), channel_id=1, source_target_pairs={{0,1},{1,0},{2,3},{3,2},{4,5},{5,4},{6,7},{7,6},{8,9},{9,8},{10,11... | collective-permute-start | bytes 1585160 | tf_op jit(solution)/shard_map/ppermute | solution.py:24
  33.7 20.3 %slice-start = ((s32[8,4,8]{2,1,0:T(4,128)}), s32[7,4,8]{2,1,0:T(4,128)S(1)}, s32[]{:S(2)}) async-start(s32[8,4,8]{2,1,0:T(4,128)} %pattern_ref.1), calls=%async_computation.3 | async-start | bytes 28672 | tf_op jit(solution)/shard_map/slice | solution.py:272
  33.7 23.0 %collective-permute-start.11 = (bf16[16,64,512]{2,1,0:T(8,128)(2,1)}, bf16[16,64,512]{2,1,0:T(8,128)(2,1)}, u32[]{:S(2)}, u32[]{:S(2)}) collective-permute-start(bf16[16,64,512]{2,1,0:T(8,128)(2,1)} %collective-permute-done.9.refs_2_), channel_id=1, source_target_pairs={{0,64},{1,17},{2,66},{3,19},{4,68},{5,21},{6,70},{7,23},{8,72},{9,... | collective-permute-start | bytes 3145736 | tf_op jit(solution)/shard_map/ppermute | solution.py:42
  43.3 15.6 %collective-permute-start.12 = (bf16[16,64,512]{2,1,0:T(8,128)(2,1)}, bf16[16,64,512]{2,1,0:T(8,128)(2,1)}, u32[]{:S(2)}, u32[]{:S(2)}) collective-permute-start(bf16[16,64,512]{2,1,0:T(8,128)(2,1)} %collective-permute-done.10.refs_5_), channel_id=1, source_target_pairs={{0,192},{1,49},{2,194},{3,51},{4,196},{5,53},{6,198},{7,55},{8,200... | collective-permute-start | bytes 3145736 | tf_op jit(solution)/shard_map/ppermute | solution.py:42
  48.7 28.6 %collective-permute-start.8 = (bf16[2064,128]{1,0:T(8,128)(2,1)}, bf16[2064,128]{1,0:T(8,128)(2,1)}, u32[]{:S(2)}, u32[]{:S(2)}) collective-permute-start(bf16[2064,128]{1,0:T(8,128)(2,1)} %fusion.1), channel_id=1, source_target_pairs={{0,4},{14,10},{1,5},{15,11},{16,20},{30,26},{17,21},{31,27},{32,36... | collective-permute-start | bytes 1585160 | tf_op jit(solution)/shard_map/ppermute | solution.py:241
  58.8 0.6 copy-start.1
  67.5 21.6 %all-to-all-start = ((f32[16,32,128]{2,1,0:T(8,128)}), f32[16,32,128]{2,1,0:T(8,128)S(1)}, u32[]{:S(2)}, u32[]{:S(2)}) async-start(f32[16,32,128]{2,1,0:T(8,128)} %bitcast.6), calls=%async_computation | async-start | bytes 524288 | tf_op jit(solution)/shard_map/all_to_all | solution.py:277
  90.0 14.8 %collective-permute-start.13 = (bf16[2064,128]{1,0:T(8,128)(2,1)S(1)}, bf16[2064,128]{1,0:T(8,128)(2,1)S(1)}, u32[]{:S(2)}, u32[]{:S(2)}) collective-permute-start(bf16[2064,128]{1,0:T(8,128)(2,1)S(1)} %broadcast_select_fusion), channel_id=1, source_target_pairs={{0,2},{4,6},{10,8},{14,12},{1,3},{5,7},{11,9},{15,13},{16,18},{20,... | collective-permute-start | bytes 1585160 | tf_op jit(solution)/shard_map/ppermute | solution.py:241
  91.4 11.5 %all-to-all-start.1 = ((bf16[16,16,128]{2,1,0:T(8,128)(2,1)}), bf16[16,16,128]{2,1,0:T(8,128)(2,1)S(1)}, u32[]{:S(2)}, u32[]{:S(2)}) async-start(bf16[16,16,128]{2,1,0:T(8,128)(2,1)} %get-tuple-element.15), calls=%async_computation.1 | async-start | bytes 131072 | tf_op jit(solution)/shard_map/all_to_all | solution.py:285
  102.9 2.8 %collective-permute-start.14 = (bf16[16,16,128]{2,1,0:T(8,128)(2,1)S(1)}, bf16[16,16,128]{2,1,0:T(8,128)(2,1)S(1)}, u32[]{:S(2)}, u32[]{:S(2)}) collective-permute-start(bf16[16,16,128]{2,1,0:T(8,128)(2,1)S(1)} %all-to-all-done.1.mine_ref), channel_id=1, source_target_pairs={{0,1},{1,0},{2,3},{3,2},{4,5},{5,4},{6,7},{7,6},{8,9},{9,8},{10,11... | collective-permute-start | bytes 196616 | tf_op jit(solution)/shard_map/ppermute | solution.py:24
  117.9 3.1 %collective-permute-start.15 = (f32[8,2,16,128]{3,2,1,0:T(8,128)S(1)}, f32[8,2,16,128]{3,2,1,0:T(8,128)S(1)}, u32[]{:S(2)}, u32[]{:S(2)}) collective-permute-start(f32[8,2,16,128]{3,2,1,0:T(8,128)S(1)} %all_to_all.15), channel_id=1, source_target_pairs={{0,1},{1,0},{2,3},{3,2},{4,5},{5,4},{6,7},{7,6},{8,9},{9,8},{10,11... | collective-permute-start | bytes 393224 | tf_op jit(solution)/shard_map/ppermute | solution.py:24

commit v3 on v2

--- a/solution.py
+++ b/solution.py
@@ -15,7 +15,7 @@
 SIDE = 2 * SLOTS * BS
 PAIR = SIDE + 16
 NT = (((1,), (1,)), ((), ()))
-VMEM_LIMIT = 48 * 1024 * 1024
+VMEM_LIMIT = 22 * 1024 * 1024
 PACK_LIMIT = 58 * 1024 * 1024
 SMALL_LIMIT = 4 * 1024 * 1024
 
@@ -95,12 +95,15 @@
     return pack[SIDE : SIDE + ROWS, :SLOTS].astype(jnp.int32)
 
 
-def picked_rows(table_ref, idx, base):
+def picked_rows(table, last, idx, base):
     parts = []
     for s in range(SLOTS):
         code = idx[base + s]
         lane = pl.multiple_of(lax.rem(code, ROWS) * BS, BS)
-        parts.append(table_ref[lax.div(code, ROWS), :, pl.ds(lane, BS)])
+        slab = lax.div(code, ROWS)
+        staged = table[jnp.minimum(slab, table.shape[0] - 1), :, pl.ds(lane, BS)]
+        beyond = last[jnp.maximum(slab - table.shape[0], 0), :, pl.ds(lane, BS)]
+        parts.append(jnp.where(slab >= table.shape[0], beyond, staged))
     return jnp.concatenate(parts, axis=1)
 
 
@@ -108,32 +111,33 @@
     return lax.dot_general(rows, jnp.concatenate(squares, axis=1), NT, preferred_element_type=F32)
 
 
-def field_kernel(now_idx, past_idx, is_last, blocks_ref, next_ref, *refs):
-    parts, (out_ref, acc, squares, table, sems) = refs[:PARTS], refs[PARTS:]
+def stage_kernel(blocks_ref, *refs):
+    parts, (table_ref, squares_ref, sems) = refs[:STAGED], refs[STAGED:]
     size = parts[0].shape[0]
-    tables = [
-        pltpu.make_async_copy(part, table.at[pl.ds(i * size, size)], sems.at[STEPS + i]) for i, part in enumerate(parts)
-    ]
-    arriving = [pltpu.make_async_copy(blocks_ref.at[k], squares.at[k], sems.at[k]) for k in range(STEPS)]
-    for copy in tables + arriving:
+    copies = [pltpu.make_async_copy(blocks_ref.at[k], squares_ref.at[k], sems.at[k]) for k in range(STEPS)]
+    for i, part in enumerate(parts):
+        copies.append(pltpu.make_async_copy(part, table_ref.at[pl.ds(i * size, size)], sems.at[STEPS + i]))
+    for copy in copies:
         copy.start()
-    for copy in tables:
+    for copy in copies:
         copy.wait()
+
+
+def field_kernel(now_idx, past_idx, is_last, squares, next_ref, table, last_ref, out_ref, acc):
     for row in range(ROWS):
-        last = picked_rows(table, past_idx, row * SLOTS)
+        last = picked_rows(table, last_ref, past_idx, row * SLOTS)
         at = (row % 2) * SLOTS
         matrix = [next_ref[row // 2, (at + s) * BS : (at + s + 1) * BS] for s in range(SLOTS)]
         acc[row, CH:] = jnp.where(is_last[0] == 1, 0.0, slot_product(last, matrix))
     for k in range(STEPS):
-        arriving[k].wait()
         for row in range(ROWS):
             base = (k * ROWS + row) * SLOTS
             matrix = [squares[k, row, s] for s in range(SLOTS)]
-            now = picked_rows(table, now_idx, base)
+            now = picked_rows(table, last_ref, now_idx, base)
             if k == 0:
                 acc[row, :CH] = slot_product(now, matrix)
             else:
-                past = picked_rows(table, past_idx, base)
+                past = picked_rows(table, last_ref, past_idx, base)
                 acc[row] += slot_product(jnp.concatenate([now, past]), matrix)
     for row in range(ROWS):
         for f in range(2):
@@ -147,25 +151,36 @@
 IN_HBM = pl.BlockSpec(memory_space=pltpu.HBM)
 ANYWHERE = pl.BlockSpec(memory_space=pl.ANY)
 SLAB = (CH, ROWS * BS)
-PARTS = 8
-
-
-def field_partials(blocks, following, parts, now_idx, past_idx, is_last):
+STAGED = 7
+
+
+def staged(blocks, parts):
+    return pl.pallas_call(
+        stage_kernel,
+        in_specs=[IN_HBM] + [ANYWHERE] * STAGED,
+        out_specs=[IN_VMEM] * 2,
+        out_shape=[
+            jax.ShapeDtypeStruct((STAGED * parts[0].shape[0], *SLAB), BF16),
+            jax.ShapeDtypeStruct(blocks.shape, BF16),
+        ],
+        scratch_shapes=[pltpu.SemaphoreType.DMA((STEPS + STAGED,))],
+        compiler_params=pltpu.CompilerParams(vmem_limit_bytes=VMEM_LIMIT),
+        cost_estimate=pl.CostEstimate(flops=0, bytes_accessed=1 << 24, transcendentals=0),
+        name="staged",
+    )(blocks, *parts)
+
+
+def field_partials(squares, following, table, last, now_idx, past_idx, is_last):
     return pl.pallas_call(
         field_kernel,
-        in_specs=[IN_SMEM] * 3 + [IN_HBM, IN_VMEM] + [ANYWHERE] * PARTS,
+        in_specs=[IN_SMEM] * 3 + [IN_VMEM] * 4,
         out_specs=IN_VMEM,
         out_shape=jax.ShapeDtypeStruct((Z, C, 2, 2, CHZ, BS), F32),
-        scratch_shapes=[
-            pltpu.VMEM((ROWS, 2 * CH, BS), F32),
-            pltpu.VMEM((STEPS, ROWS, SLOTS, BS, BS), BF16),
-            pltpu.VMEM((Y * X * STEPS, *SLAB), BF16),
-            pltpu.SemaphoreType.DMA((STEPS + PARTS,)),
-        ],
+        scratch_shapes=[pltpu.VMEM((ROWS, 2 * CH, BS), F32)],
         compiler_params=pltpu.CompilerParams(vmem_limit_bytes=VMEM_LIMIT),
         cost_estimate=pl.CostEstimate(flops=1 << 30, bytes_accessed=1 << 24, transcendentals=0),
         name="field_partials",
-    )(now_idx, past_idx, is_last, blocks, following, *parts)
+    )(now_idx, past_idx, is_last, squares, following, table, last)
 
 
 def exact_dot(a, b):
@@ -258,7 +273,7 @@
     below = hop(line[0], 1, 1)
     above = hop(line[1], 1, -1)
     below_rest = hop(line[1], 1, 1)
-    above_rest = hop(line[0], 1, -1)
+    above_rest = hop(after(line[0], below), 1, -1)
     far = hop(below, 1, 1), hop(above, 1, -1)
     following = lax.ppermute(pack, ("z", "core"), [(i, (i - 1) % bands) for i in range(bands)])
     given = jnp.where(core == 0, pack[1], following[0])
@@ -271,16 +286,16 @@
     now_idx = entries(pattern, steps)
     past_cols = jnp.concatenate([packed_codes(following[0])[None], pattern[1:]])
     past_idx = entries(past_cols, (steps - 1) % STEPS)
-    parts = (*line, below, below_rest, above_rest, above, *far)
     is_last = (z * C + core == bands - 1).astype(jnp.int32).reshape(1)
-    partial = field_partials(blocks, following, parts, now_idx.reshape(-1), past_idx.reshape(-1), is_last)
+    table, squares = staged(blocks, (*line, below, below_rest, above_rest, above, far[0]))
+    partial = field_partials(squares, following, table, far[1], now_idx.reshape(-1), past_idx.reshape(-1), is_last)
     parts = lax.all_to_all(partial.reshape(Z * C, 4 * CHZ, BS), ("z", "core"), 0, 0)
 
     excite = lax.dynamic_slice(excitation, (0, z * CHZ, core * 2 * BS), (2, CHZ, 2 * BS))
     excite = excite.reshape(2, CHZ, 2, BS).transpose(0, 2, 1, 3)
     near = lax.dynamic_slice(near_inverse, (core * 2, 0, 0), (2, BS, BS))
     current, low, rest = first_solve(parts, excite, near)
-    front = spread(front, 1, lambda new: after(new, current))
+    front = spread(front, 1, lambda new: new)
 
     mine = lax.all_to_all(low, ("y", "x"), 0, 0)
     other = swap_cores(mine)

time: 123 us -> 121 us (0.984)
  starting transfers between devices: 51.8 us -> 47.5 us
  other arithmetic: 6.59 us -> 3.4 us
  waiting for transfers between devices: 29.3 us -> 32.4 us
  Pallas kernels: 13.3 us -> 15.3 us
    ppermute x10, waiting for transfers between devices: 10.5 us -> 16.7 us  [hop(): return lax.ppermute(array, ('y', 'x', 'z', 'core'), hop_pairs(phase, by))]
    unnamed x15 -> x19, local copies, waits for them, and re-layouts: 2.72 us -> 7.7 us
    all_to_all x1, waiting for transfers between devices: 10.6 us -> 6.51 us  [local(): lax.all_to_all(partial.reshape(Z * C, 4 * CHZ, BS), ('z', 'core'), 0, 0)]
    ppermute x10, starting transfers between devices: 16.6 us -> 14.3 us  [hop(): return lax.ppermute(array, ('y', 'x', 'z', 'core'), hop_pairs(phase, by))]
    pallas_call x1 -> x2, Pallas kernels: 8 us -> 9.95 us  [the longest x1 6.93 us: field_partials(): pl.pallas_call(field_kernel, in_specs=[IN_SMEM] * 3 + [IN_VMEM] * 4, out_...]
    ppermute x3, starting transfers between devices: 10.8 us -> 8.99 us  [swap_cores(): return lax.ppermute(array, 'core', [(0, 1), (1, 0)])]
    concatenate x1, local copies, waits for them, and re-layouts: 1.41 us -> 0.09 us  [local(): past_cols = jnp.concatenate([packed_codes(following[0])[None], pattern[1:]])]
    add x2, other arithmetic: 1.43 us -> 0.14 us  [entries(): return (slot * STEPS + steps) * ROWS + cols % ROWS]
  transfers between devices with their start and end apart: 18 -> 18, of which waited for: 7 -> 11; matrix products, arithmetic and copies ran while one was open for 12% -> 6% of each run, Pallas kernels for 9% -> 12%
where the time goes in v3:
time: 121 us; the launch traced here: 120 us
  starting transfers between devices  47.5 us (39%)
  waiting for transfers between devices  32.4 us (27%)
  Pallas kernels  15.3 us (13%)
  blocking collectives  10.7 us (9%)
  local copies, waits for them, and re-layouts  10.5 us (9%)
  other arithmetic  3.4 us (3%)
    ppermute x10, waiting for transfers between devices, hop(): return lax.ppermute(array, ('y', 'x', 'z', 'core'), hop_pairs(phase, by))  16.7 us
    ppermute x10, starting transfers between devices, hop(): return lax.ppermute(array, ('y', 'x', 'z', 'core'), hop_pairs(phase, by))  14.3 us
    all_to_all x1, blocking collectives, local(): kept = lax.all_to_all(ready, 'z', 0, 0)  10.7 us
    ppermute x3, starting transfers between devices, swap_cores(): return lax.ppermute(array, 'core', [(0, 1), (1, 0)])  8.99 us
    all_to_all x1, starting transfers between devices, local(): lax.all_to_all(partial.reshape(Z * C, 4 * CHZ, BS), ('z', 'core'), 0, 0)  8.6 us
    ppermute x2, starting transfers between devices, spread(): received = lax.ppermute(tie(array), 'z', SPREAD[step])  8 us
    unnamed x19, local copies, waits for them, and re-layouts  7.7 us
    pallas_call x1, Pallas kernels, field_partials(): pl.pallas_call(field_kernel, in_specs=[IN_SMEM] * 3 + [IN_VMEM] * 4, out_...  6.93 us
  transfers between devices with their start and end apart: 18, of which 11 were waited for; matrix products, arithmetic and copies ran while one was open for 6% of the time, Pallas kernels for 12%

profile of v3, /device:TPU:1, one launch (start us, length us, event | category | flops | bytes accessed | tf_op | source)
XLA Modules:
  0.0 120.0 jit_solution(13705425111873990016)
XLA Ops:
  0.0 2.1 %collective-permute-start.3 = (bf16[8,64,512]{2,1,0:T(8,128)(2,1)}, bf16[8,64,512]{2,1,0:T(8,128)(2,1)S(1)}, u32[]{:S(2)}, u32[]{:S(2)}) collective-permute-start(bf16[8,64,512]{2,1,0:T(8,128)(2,1)} %param.6), channel_id=1, source_target_pairs={{0,16},{1,65},{2,18},{3,67},{4,20},{5,69},{6,22},{7,71},{8,24},{9,... | collective-permute-start | bytes 1572872 | tf_op jit(solution)/shard_map/ppermute | solution.py:42
  2.1 1.5 %collective-permute-start.2 = (bf16[8,64,512]{2,1,0:T(8,128)(2,1)}, bf16[8,64,512]{2,1,0:T(8,128)(2,1)S(1)}, u32[]{:S(2)}, u32[]{:S(2)}) collective-permute-start(bf16[8,64,512]{2,1,0:T(8,128)(2,1)} %param.6), channel_id=1, source_target_pairs={{0,48},{1,193},{2,50},{3,195},{4,52},{5,197},{6,54},{7,199},{8,56}... | collective-permute-start | bytes 1572872 | tf_op jit(solution)/shard_map/ppermute | solution.py:42
  3.7 3.1 %packed_front.1 = bf16[2,2064,128]{2,1,0:T(8,128)(2,1)} custom-call(bf16[32768,128]{1,0:T(8,128)(2,1)} %bitcast.31, s32[8,4,8]{2,1,0:T(4,128)} %pattern_ref.1), custom_call_target="tpu_custom_call" | custom-call | tf_op jit(solution)/shard_map/packed_front/pallas_call | solution.py:83
  6.8 2.8 %collective-permute-start = (bf16[2,2064,128]{2,1,0:T(8,128)(2,1)}, bf16[2,2064,128]{2,1,0:T(8,128)(2,1)S(1)}, u32[]{:S(2)}, u32[]{:S(2)}) collective-permute-start(bf16[2,2064,128]{2,1,0:T(8,128)(2,1)} %packed_front.1), channel_id=1, source_target_pairs={{0,15},{1,0},{2,1},{3,2},{4,3},{5,4},{6,5},{7,6},{8,7},{9,8},{10,9... | collective-permute-start | bytes 3170312 | tf_op jit(solution)/shard_map/ppermute | solution.py:278
  9.7 1.0 collective-permute-done.3
  10.6 0.7 slice.41
  11.5 0.1 add.153
  11.6 2.7 %collective-permute-start.5 = (bf16[4,64,512]{2,1,0:T(8,128)(2,1)S(1)}, bf16[4,64,512]{2,1,0:T(8,128)(2,1)S(1)}, u32[]{:S(2)}, u32[]{:S(2)}) collective-permute-start(bf16[4,64,512]{2,1,0:T(8,128)(2,1)S(1)} %slice.42), channel_id=1, source_target_pairs={{0,48},{1,193},{2,50},{3,195},{4,52},{5,197},{6,54},{7,199},{8,56}... | collective-permute-start | bytes 786440 | tf_op jit(solution)/shard_map/ppermute | solution.py:42
  14.4 1.0 collective-permute-start.7
  15.4 1.1 constant_dynamic-update-slice_fusion.2
  16.5 1.6 %collective-permute-done.4 = bf16[4,64,512]{2,1,0:T(8,128)(2,1)} collective-permute-done((bf16[4,64,512]{2,1,0:T(8,128)(2,1)}, bf16[4,64,512]{2,1,0:T(8,128)(2,1)}, u32[]{:S(2)}, u32[]{:S(2)}) %collective-permute-start.4) | collective-permute-done | bytes 262176 | tf_op jit(solution)/shard_map/ppermute | solution.py:42
  18.1 1.0 constant_dynamic-update-slice_fusion.1
  19.1 2.6 %collective-permute-start.11 = (bf16[16,64,512]{2,1,0:T(8,128)(2,1)S(1)}, bf16[16,64,512]{2,1,0:T(8,128)(2,1)}, u32[]{:S(2)}, u32[]{:S(2)}) collective-permute-start(bf16[16,64,512]{2,1,0:T(8,128)(2,1)S(1)} %constant_dynamic-update-slice_fusion.refs_1_), channel_id=1, source_target_pairs={{0,192},{1,49},{2,194},{3,51},{4,196},{5,53},{6,198},{7,55},{8,200... | collective-permute-start | bytes 3145736 | tf_op jit(solution)/shard_map/ppermute | solution.py:42
  21.7 0.1 fusion.9
  21.8 0.1 reshape.57.now_idx
  21.9 0.7 collective-permute-done.next_ref
  22.6 1.1 fusion.2
  23.7 6.2 %collective-permute-start.1 = (bf16[2064,128]{1,0:T(8,128)(2,1)S(1)}, bf16[2064,128]{1,0:T(8,128)(2,1)S(1)}, u32[]{:S(2)}, u32[]{:S(2)}) collective-permute-start(bf16[2064,128]{1,0:T(8,128)(2,1)S(1)} %fusion.2), channel_id=1, source_target_pairs={{0,1},{1,0},{2,3},{3,2},{4,5},{5,4},{6,7},{7,6},{8,9},{9,8},{10,11... | collective-permute-start | bytes 1585160 | tf_op jit(solution)/shard_map/ppermute | solution.py:24
  29.9 2.7 %collective-permute-done.7.refs_2_ = bf16[16,64,512]{2,1,0:T(8,128)(2,1)} collective-permute-done((bf16[16,64,512]{2,1,0:T(8,128)(2,1)S(1)}, bf16[16,64,512]{2,1,0:T(8,128)(2,1)}, u32[]{:S(2)}, u32[]{:S(2)}) %collective-permute-start.7) | collective-permute-done | bytes 1048608 | tf_op jit(solution)/shard_map/ppermute | solution.py:42
  32.6 1.0 collective-permute-start.8
  33.6 0.6 collective-permute-start.12
  34.2 2.8 %collective-permute-start.13 = (bf16[16,64,512]{2,1,0:T(8,128)(2,1)}, bf16[16,64,512]{2,1,0:T(8,128)(2,1)}, u32[]{:S(2)}, u32[]{:S(2)}) collective-permute-start(bf16[16,64,512]{2,1,0:T(8,128)(2,1)} %collective-permute-done.11.refs_5_), channel_id=1, source_target_pairs={{0,192},{1,49},{2,194},{3,51},{4,196},{5,53},{6,198},{7,55},{8,200... | collective-permute-start | bytes 3145736 | tf_op jit(solution)/shard_map/ppermute | solution.py:42
  36.9 0.9 fusion.1
  37.8 6.0 %collective-permute-done.6.refs_3_ = bf16[16,64,512]{2,1,0:T(8,128)(2,1)} collective-permute-done((bf16[16,64,512]{2,1,0:T(8,128)(2,1)S(1)}, bf16[16,64,512]{2,1,0:T(8,128)(2,1)}, u32[]{:S(2)}, u32[]{:S(2)}) %collective-permute-start.6) | collective-permute-done | bytes 1048608 | tf_op jit(solution)/shard_map/ppermute | solution.py:42
  43.8 2.8 %collective-permute-done.8.refs_4_ = bf16[16,64,512]{2,1,0:T(8,128)(2,1)S(1)} collective-permute-done((bf16[16,64,512]{2,1,0:T(8,128)(2,1)S(1)}, bf16[16,64,512]{2,1,0:T(8,128)(2,1)S(1)}, u32[]{:S(2)}, u32[]{:S(2)}) %collective-permute-start.8) | collective-permute-done | bytes 1048608 | tf_op jit(solution)/shard_map/ppermute | solution.py:42
  46.6 1.0 copy-done.2
  47.6 4.7 %collective-permute-start.9 = (bf16[2064,128]{1,0:T(8,128)(2,1)}, bf16[2064,128]{1,0:T(8,128)(2,1)}, u32[]{:S(2)}, u32[]{:S(2)}) collective-permute-start(bf16[2064,128]{1,0:T(8,128)(2,1)} %fusion.1), channel_id=1, source_target_pairs={{0,4},{14,10},{1,5},{15,11},{16,20},{30,26},{17,21},{31,27},{32,36... | collective-permute-start | bytes 1585160 | tf_op jit(solution)/shard_map/ppermute | solution.py:256
  52.3 0.1 concatenate.15
  52.4 2.6 %collective-permute-done.12.refs_6_ = bf16[16,64,512]{2,1,0:T(8,128)(2,1)} collective-permute-done((bf16[16,64,512]{2,1,0:T(8,128)(2,1)}, bf16[16,64,512]{2,1,0:T(8,128)(2,1)}, u32[]{:S(2)}, u32[]{:S(2)}) %collective-permute-start.12) | collective-permute-done | bytes 1048608 | tf_op jit(solution)/shard_map/ppermute | solution.py:42
  55.0 3.4 %copy-done.1 = bf16[8,4,8,128,128]{4,3,2,1,0:T(8,128)(2,1)S(1)} copy-done((bf16[8,4,8,128,128]{4,3,2,1,0:T(8,128)(2,1)S(1)}, bf16[8,4,8,128,128]{4,3,2,1,0:T(8,128)(2,1)}, u32[]{:S(2)}) %copy-start.1) | copy-done | bytes 8388632
  58.4 1.2 %copy-done.3 = bf16[16,64,512]{2,1,0:T(8,128)(2,1)S(1)} copy-done((bf16[16,64,512]{2,1,0:T(8,128)(2,1)S(1)}, bf16[16,64,512]{2,1,0:T(8,128)(2,1)}, u32[]{:S(2)}) %copy-start.3) | copy-done | bytes 1048600
  59.7 3.0 %staged.1 = (bf16[112,64,512]{2,1,0:T(8,128)(2,1)S(1)}, bf16[8,4,8,128,128]{4,3,2,1,0:T(8,128)(2,1)S(1)}) custom-call(bf16[8,4,8,128,128]{4,3,2,1,0:T(8,128)(2,1)S(1)} %copy-done.1, bf16[16,64,512]{2,1,0:T(8,128)(2,1)S(1)} %constant_dynamic-update-slice_fusion.3.refs_0_, bf16[16,64,512]{2,1,0:T(8,128)(2,1)S(1)} %constant_dynamic-update-slice_fusion.refs_1_, ...), custom_call_target="tpu_custom_call" | custom-call | bytes 16777216 | tf_op jit(solution)/shard_map/staged/pallas_call | solution.py:158
  62.7 6.9 %field_partials.1 = f32[8,2,2,2,8,128]{5,4,3,2,1,0:T(8,128)} custom-call(s32[256]{0:T(256)S(1)} %reshape.57.now_idx, s32[256]{0:T(256)S(1)} %fusion.11.past_idx, s32[1]{0:T(128)} %bitcast.5.is_last, bf16[8,4,8,128,128]{4,3,2,1,0:T(8,128)(2,1)S(1)} %get-tuple-element.16.squares, bf16[2,2064,128]{2,1,0:T(8,128)(2,1)S(1)} %collective-permute-done.next_ref, ...), custom_call_target="tpu_custom_call" | custom-call | flops 1073741824 | bytes 16777216 | tf_op jit(solution)/shard_map/field_partials/pallas_call | solution.py:174
  69.6 8.6 %all-to-all-start = ((f32[16,32,128]{2,1,0:T(8,128)}), f32[16,32,128]{2,1,0:T(8,128)S(1)}, u32[]{:S(2)}, u32[]{:S(2)}) async-start(f32[16,32,128]{2,1,0:T(8,128)} %bitcast.6), calls=%async_computation | async-start | bytes 524288 | tf_op jit(solution)/shard_map/all_to_all | solution.py:292
  78.2 1.1 broadcast_select_fusion
  79.3 3.3 %collective-permute-start.10 = (bf16[2064,128]{1,0:T(8,128)(2,1)S(1)}, bf16[2064,128]{1,0:T(8,128)(2,1)S(1)}, u32[]{:S(2)}, u32[]{:S(2)}) collective-permute-start(bf16[2064,128]{1,0:T(8,128)(2,1)S(1)} %broadcast_select_fusion), channel_id=1, source_target_pairs={{0,2},{4,6},{10,8},{14,12},{1,3},{5,7},{11,9},{15,13},{16,18},{20,... | collective-permute-start | bytes 1585160 | tf_op jit(solution)/shard_map/ppermute | solution.py:256
  82.7 0.7 dynamic-slice_bitcast_fusion.excite_ref
  83.4 6.5 %all-to-all-done.parts_ref = f32[16,32,128]{2,1,0:T(8,128)S(1)} async-done(((f32[16,32,128]{2,1,0:T(8,128)}), f32[16,32,128]{2,1,0:T(8,128)S(1)}, u32[]{:S(2)}, u32[]{:S(2)}) %all-to-all-start) | async-done | bytes 262176 | tf_op jit(solution)/shard_map/all_to_all | solution.py:292
  89.9 1.0 first_solve.1
  90.9 4.8 %all-to-all-start.1 = ((bf16[16,16,128]{2,1,0:T(8,128)(2,1)}), bf16[16,16,128]{2,1,0:T(8,128)(2,1)S(1)}, u32[]{:S(2)}, u32[]{:S(2)}) async-start(bf16[16,16,128]{2,1,0:T(8,128)(2,1)} %get-tuple-element.18), calls=%async_computation.1 | async-start | bytes 131072 | tf_op jit(solution)/shard_map/all_to_all | solution.py:300
  95.7 6.8 %all-to-all-done.1.mine_ref = bf16[16,16,128]{2,1,0:T(8,128)(2,1)S(1)} async-done(((bf16[16,16,128]{2,1,0:T(8,128)(2,1)}), bf16[16,16,128]{2,1,0:T(8,128)(2,1)S(1)}, u32[]{:S(2)}, u32[]{:S(2)}) %all-to-all-start.1) | async-done | bytes 65568 | tf_op jit(solution)/shard_map/all_to_all | solution.py:300
  102.5 0.7 collective-permute-start.14
  103.5 0.7 collective-permute-done.14.other_ref
  104.1 1.3 %second_solve.1 = f32[8,2,16,128]{3,2,1,0:T(8,128)S(1)} custom-call(s32[16]{0:T(128)S(1)} %fusion.16.idx, bf16[16,16,128]{2,1,0:T(8,128)(2,1)S(1)} %all-to-all-done.1.mine_ref, bf16[16,16,128]{2,1,0:T(8,128)(2,1)S(1)} %collective-permute-done.14.other_ref, bf16[2064,128]{1,0:T(8,128)(2,1)S(1)} %broadcast_select_fusion.1.blocks_ref, ...), custom_call_target="tpu_custom_call" | custom-call | tf_op jit(solution)/shard_map/second_solve/pallas_call | solution.py:240
  105.4 10.7 %all_to_all.15 = f32[8,2,16,128]{3,2,1,0:T(8,128)S(1)} all-to-all(f32[8,2,16,128]{3,2,1,0:T(8,128)S(1)} %second_solve.1), channel_id=1, replica_groups=mesh['y'=4,'x'=4,'z'=8,'core'=2] {'z'}, dimensions={0} | all-to-all | bytes 262144 | tf_op jit(solution)/shard_map/all_to_all | solution.py:306
  116.1 2.1 %collective-permute-start.15 = (f32[8,2,16,128]{3,2,1,0:T(8,128)S(1)}, f32[8,2,16,128]{3,2,1,0:T(8,128)S(1)}, u32[]{:S(2)}, u32[]{:S(2)}) collective-permute-start(f32[8,2,16,128]{3,2,1,0:T(8,128)S(1)} %all_to_all.15), channel_id=1, source_target_pairs={{0,1},{1,0},{2,3},{3,2},{4,5},{5,4},{6,7},{7,6},{8,9},{9,8},{10,11... | collective-permute-start | bytes 393224 | tf_op jit(solution)/shard_map/ppermute | solution.py:24
  118.2 1.0 collective-permute-done.15
  119.3 0.7 copy.6
  (42 shorter events, 0.6 us)
Async XLA Ops:
  0.0 83.4 %copy-start = (f32[4,128,128]{2,1,0:T(8,128)S(1)}, f32[4,128,128]{2,1,0:T(8,128)}, u32[]{:S(2)}) copy-start(f32[4,128,128]{2,1,0:T(8,128)} %param.9) | copy-start | bytes 786436
  0.0 10.6 %collective-permute-start.3 = (bf16[8,64,512]{2,1,0:T(8,128)(2,1)}, bf16[8,64,512]{2,1,0:T(8,128)(2,1)S(1)}, u32[]{:S(2)}, u32[]{:S(2)}) collective-permute-start(bf16[8,64,512]{2,1,0:T(8,128)(2,1)} %param.6), channel_id=1, source_target_pairs={{0,16},{1,65},{2,18},{3,67},{4,20},{5,69},{6,22},{7,71},{8,24},{9,... | collective-permute-start | bytes 1572872 | tf_op jit(solution)/shard_map/ppermute | solution.py:42
  2.1 9.5 %collective-permute-start.2 = (bf16[8,64,512]{2,1,0:T(8,128)(2,1)}, bf16[8,64,512]{2,1,0:T(8,128)(2,1)S(1)}, u32[]{:S(2)}, u32[]{:S(2)}) collective-permute-start(bf16[8,64,512]{2,1,0:T(8,128)(2,1)} %param.6), channel_id=1, source_target_pairs={{0,48},{1,193},{2,50},{3,195},{4,52},{5,197},{6,54},{7,199},{8,56}... | collective-permute-start | bytes 1572872 | tf_op jit(solution)/shard_map/ppermute | solution.py:42
  3.7 6.0 %copy-start.6 = (bf16[8,64,512]{2,1,0:T(8,128)(2,1)S(1)}, bf16[8,64,512]{2,1,0:T(8,128)(2,1)}, u32[]{:S(2)}) copy-start(bf16[8,64,512]{2,1,0:T(8,128)(2,1)} %param.6) | copy-start | bytes 1572868
  6.8 15.8 %collective-permute-start = (bf16[2,2064,128]{2,1,0:T(8,128)(2,1)}, bf16[2,2064,128]{2,1,0:T(8,128)(2,1)S(1)}, u32[]{:S(2)}, u32[]{:S(2)}) collective-permute-start(bf16[2,2064,128]{2,1,0:T(8,128)(2,1)} %packed_front.1), channel_id=1, source_target_pairs={{0,15},{1,0},{2,1},{3,2},{4,3},{5,4},{6,5},{7,6},{8,7},{9,8},{10,9... | collective-permute-start | bytes 3170312 | tf_op jit(solution)/shard_map/ppermute | solution.py:278
  11.4 6.7 %collective-permute-start.4 = (bf16[4,64,512]{2,1,0:T(8,128)(2,1)}, bf16[4,64,512]{2,1,0:T(8,128)(2,1)}, u32[]{:S(2)}, u32[]{:S(2)}) collective-permute-start(bf16[4,64,512]{2,1,0:T(8,128)(2,1)} %slice.41), channel_id=1, source_target_pairs={{0,16},{1,65},{2,18},{3,67},{4,20},{5,69},{6,22},{7,71},{8,24},{9,... | collective-permute-start | bytes 786440 | tf_op jit(solution)/shard_map/ppermute | solution.py:42
  11.6 2.8 %copy-start.5 = (bf16[8,64,512]{2,1,0:T(8,128)(2,1)}, bf16[8,64,512]{2,1,0:T(8,128)(2,1)S(1)}, u32[]{:S(2)}) copy-start(bf16[8,64,512]{2,1,0:T(8,128)(2,1)S(1)} %collective-permute-done.2) | copy-start | bytes 1572868
  11.6 7.4 %collective-permute-start.5 = (bf16[4,64,512]{2,1,0:T(8,128)(2,1)S(1)}, bf16[4,64,512]{2,1,0:T(8,128)(2,1)S(1)}, u32[]{:S(2)}, u32[]{:S(2)}) collective-permute-start(bf16[4,64,512]{2,1,0:T(8,128)(2,1)S(1)} %slice.42), channel_id=1, source_target_pairs={{0,48},{1,193},{2,50},{3,195},{4,52},{5,197},{6,54},{7,199},{8,56}... | collective-permute-start | bytes 786440 | tf_op jit(solution)/shard_map/ppermute | solution.py:42
  14.4 7.3 %copy-start.7 = (s32[8,4,8]{2,1,0:T(4,128)S(1)}, s32[8,4,8]{2,1,0:T(4,128)}, u32[]{:S(2)}) copy-start(s32[8,4,8]{2,1,0:T(4,128)} %pattern_ref.1) | copy-start | bytes 3076
  14.4 18.1 %collective-permute-start.7 = (bf16[16,64,512]{2,1,0:T(8,128)(2,1)S(1)}, bf16[16,64,512]{2,1,0:T(8,128)(2,1)}, u32[]{:S(2)}, u32[]{:S(2)}) collective-permute-start(bf16[16,64,512]{2,1,0:T(8,128)(2,1)S(1)} %constant_dynamic-update-slice_fusion.3.refs_0_), channel_id=1, source_target_pairs={{0,64},{1,17},{2,66},{3,19},{4,68},{5,21},{6,70},{7,23},{8,72},{9,... | collective-permute-start | bytes 3145736 | tf_op jit(solution)/shard_map/ppermute | solution.py:42
  19.1 15.1 %collective-permute-start.11 = (bf16[16,64,512]{2,1,0:T(8,128)(2,1)S(1)}, bf16[16,64,512]{2,1,0:T(8,128)(2,1)}, u32[]{:S(2)}, u32[]{:S(2)}) collective-permute-start(bf16[16,64,512]{2,1,0:T(8,128)(2,1)S(1)} %constant_dynamic-update-slice_fusion.refs_1_), channel_id=1, source_target_pairs={{0,192},{1,49},{2,194},{3,51},{4,196},{5,53},{6,198},{7,55},{8,200... | collective-permute-start | bytes 3145736 | tf_op jit(solution)/shard_map/ppermute | solution.py:42
  21.7 22.1 %collective-permute-start.6 = (bf16[16,64,512]{2,1,0:T(8,128)(2,1)S(1)}, bf16[16,64,512]{2,1,0:T(8,128)(2,1)}, u32[]{:S(2)}, u32[]{:S(2)}) collective-permute-start(bf16[16,64,512]{2,1,0:T(8,128)(2,1)S(1)} %constant_dynamic-update-slice_fusion.refs_1_), channel_id=1, source_target_pairs={{0,64},{1,17},{2,66},{3,19},{4,68},{5,21},{6,70},{7,23},{8,72},{9,... | collective-permute-start | bytes 3145736 | tf_op jit(solution)/shard_map/ppermute | solution.py:42
  21.9 15.1 %copy-start.4 = (bf16[2,2064,128]{2,1,0:T(8,128)(2,1)S(1)}, bf16[2,2064,128]{2,1,0:T(8,128)(2,1)}, u32[]{:S(2)}) copy-start(bf16[2,2064,128]{2,1,0:T(8,128)(2,1)} %packed_front.1) | copy-start | bytes 3170308
  23.7 13.2 %collective-permute-start.1 = (bf16[2064,128]{1,0:T(8,128)(2,1)S(1)}, bf16[2064,128]{1,0:T(8,128)(2,1)S(1)}, u32[]{:S(2)}, u32[]{:S(2)}) collective-permute-start(bf16[2064,128]{1,0:T(8,128)(2,1)S(1)} %fusion.2), channel_id=1, source_target_pairs={{0,1},{1,0},{2,3},{3,2},{4,5},{5,4},{6,7},{7,6},{8,9},{9,8},{10,11... | collective-permute-start | bytes 1585160 | tf_op jit(solution)/shard_map/ppermute | solution.py:24
  32.6 14.0 %collective-permute-start.8 = (bf16[16,64,512]{2,1,0:T(8,128)(2,1)S(1)}, bf16[16,64,512]{2,1,0:T(8,128)(2,1)S(1)}, u32[]{:S(2)}, u32[]{:S(2)}) collective-permute-start(bf16[16,64,512]{2,1,0:T(8,128)(2,1)S(1)} %constant_dynamic-update-slice_fusion.3.refs_0_), channel_id=1, source_target_pairs={{0,192},{1,49},{2,194},{3,51},{4,196},{5,53},{6,198},{7,55},{8,200... | collective-permute-start | bytes 3145736 | tf_op jit(solution)/shard_map/ppermute | solution.py:42
  33.6 18.7 %slice-start = ((s32[8,4,8]{2,1,0:T(4,128)}), s32[7,4,8]{2,1,0:T(4,128)S(1)}, s32[]{:S(2)}) async-start(s32[8,4,8]{2,1,0:T(4,128)} %pattern_ref.1), calls=%async_computation.3 | async-start | bytes 28672 | tf_op jit(solution)/shard_map/slice | solution.py:287
  33.6 21.4 %collective-permute-start.12 = (bf16[16,64,512]{2,1,0:T(8,128)(2,1)}, bf16[16,64,512]{2,1,0:T(8,128)(2,1)}, u32[]{:S(2)}, u32[]{:S(2)}) collective-permute-start(bf16[16,64,512]{2,1,0:T(8,128)(2,1)} %collective-permute-done.7.refs_2_), channel_id=1, source_target_pairs={{0,64},{1,17},{2,66},{3,19},{4,68},{5,21},{6,70},{7,23},{8,72},{9,... | collective-permute-start | bytes 3145736 | tf_op jit(solution)/shard_map/ppermute | solution.py:42
  34.2 28.5 %collective-permute-start.13 = (bf16[16,64,512]{2,1,0:T(8,128)(2,1)}, bf16[16,64,512]{2,1,0:T(8,128)(2,1)}, u32[]{:S(2)}, u32[]{:S(2)}) collective-permute-start(bf16[16,64,512]{2,1,0:T(8,128)(2,1)} %collective-permute-done.11.refs_5_), channel_id=1, source_target_pairs={{0,192},{1,49},{2,194},{3,51},{4,196},{5,53},{6,198},{7,55},{8,200... | collective-permute-start | bytes 3145736 | tf_op jit(solution)/shard_map/ppermute | solution.py:42
  46.6 1.0 copy-start.2
  47.6 30.6 %collective-permute-start.9 = (bf16[2064,128]{1,0:T(8,128)(2,1)}, bf16[2064,128]{1,0:T(8,128)(2,1)}, u32[]{:S(2)}, u32[]{:S(2)}) collective-permute-start(bf16[2064,128]{1,0:T(8,128)(2,1)} %fusion.1), channel_id=1, source_target_pairs={{0,4},{14,10},{1,5},{15,11},{16,20},{30,26},{17,21},{31,27},{32,36... | collective-permute-start | bytes 1585160 | tf_op jit(solution)/shard_map/ppermute | solution.py:256
  55.0 3.4 %copy-start.1 = (bf16[8,4,8,128,128]{4,3,2,1,0:T(8,128)(2,1)S(1)}, bf16[8,4,8,128,128]{4,3,2,1,0:T(8,128)(2,1)}, u32[]{:S(2)}) copy-start(bf16[8,4,8,128,128]{4,3,2,1,0:T(8,128)(2,1)} %blocks_ref.1) | copy-start | bytes 25165828
  58.4 1.2 %copy-start.3 = (bf16[16,64,512]{2,1,0:T(8,128)(2,1)S(1)}, bf16[16,64,512]{2,1,0:T(8,128)(2,1)}, u32[]{:S(2)}) copy-start(bf16[16,64,512]{2,1,0:T(8,128)(2,1)} %copy-done.2) | copy-start | bytes 3145732
  69.6 20.3 %all-to-all-start = ((f32[16,32,128]{2,1,0:T(8,128)}), f32[16,32,128]{2,1,0:T(8,128)S(1)}, u32[]{:S(2)}, u32[]{:S(2)}) async-start(f32[16,32,128]{2,1,0:T(8,128)} %bitcast.6), calls=%async_computation | async-start | bytes 524288 | tf_op jit(solution)/shard_map/all_to_all | solution.py:292
  79.3 23.9 %collective-permute-start.10 = (bf16[2064,128]{1,0:T(8,128)(2,1)S(1)}, bf16[2064,128]{1,0:T(8,128)(2,1)S(1)}, u32[]{:S(2)}, u32[]{:S(2)}) collective-permute-start(bf16[2064,128]{1,0:T(8,128)(2,1)S(1)} %broadcast_select_fusion), channel_id=1, source_target_pairs={{0,2},{4,6},{10,8},{14,12},{1,3},{5,7},{11,9},{15,13},{16,18},{20,... | collective-permute-start | bytes 1585160 | tf_op jit(solution)/shard_map/ppermute | solution.py:256
  90.9 11.6 %all-to-all-start.1 = ((bf16[16,16,128]{2,1,0:T(8,128)(2,1)}), bf16[16,16,128]{2,1,0:T(8,128)(2,1)S(1)}, u32[]{:S(2)}, u32[]{:S(2)}) async-start(bf16[16,16,128]{2,1,0:T(8,128)(2,1)} %get-tuple-element.18), calls=%async_computation.1 | async-start | bytes 131072 | tf_op jit(solution)/shard_map/all_to_all | solution.py:300
  102.5 1.6 %collective-permute-start.14 = (bf16[16,16,128]{2,1,0:T(8,128)(2,1)S(1)}, bf16[16,16,128]{2,1,0:T(8,128)(2,1)S(1)}, u32[]{:S(2)}, u32[]{:S(2)}) collective-permute-start(bf16[16,16,128]{2,1,0:T(8,128)(2,1)S(1)} %all-to-all-done.1.mine_ref), channel_id=1, source_target_pairs={{0,1},{1,0},{2,3},{3,2},{4,5},{5,4},{6,7},{7,6},{8,9},{9,8},{10,11... | collective-permute-start | bytes 196616 | tf_op jit(solution)/shard_map/ppermute | solution.py:24
  116.1 3.1 %collective-permute-start.15 = (f32[8,2,16,128]{3,2,1,0:T(8,128)S(1)}, f32[8,2,16,128]{3,2,1,0:T(8,128)S(1)}, u32[]{:S(2)}, u32[]{:S(2)}) collective-permute-start(f32[8,2,16,128]{3,2,1,0:T(8,128)S(1)} %all_to_all.15), channel_id=1, source_target_pairs={{0,1},{1,0},{2,3},{3,2},{4,5},{5,4},{6,7},{7,6},{8,9},{9,8},{10,11... | collective-permute-start | bytes 393224 | tf_op jit(solution)/shard_map/ppermute | solution.py:24

commit v4 on v3

--- a/solution.py
+++ b/solution.py
@@ -103,7 +103,7 @@
         slab = lax.div(code, ROWS)
         staged = table[jnp.minimum(slab, table.shape[0] - 1), :, pl.ds(lane, BS)]
         beyond = last[jnp.maximum(slab - table.shape[0], 0), :, pl.ds(lane, BS)]
-        parts.append(jnp.where(slab >= table.shape[0], beyond, staged))
+        parts.append(lax.select(slab >= table.shape[0], beyond, staged))
     return jnp.concatenate(parts, axis=1)
 
 

time: 121 us -> 121 us (level)
  no operation moved by 1% of the time
where the time goes in v4:
time: 121 us; the launch traced here: 120 us
  starting transfers between devices  47.5 us (39%)
  waiting for transfers between devices  32.4 us (27%)
  Pallas kernels  15.3 us (13%)
  blocking collectives  10.7 us (9%)
  local copies, waits for them, and re-layouts  10.5 us (9%)
  other arithmetic  3.4 us (3%)
    ppermute x10, waiting for transfers between devices, hop(): return lax.ppermute(array, ('y', 'x', 'z', 'core'), hop_pairs(phase, by))  16.7 us
    ppermute x10, starting transfers between devices, hop(): return lax.ppermute(array, ('y', 'x', 'z', 'core'), hop_pairs(phase, by))  14.3 us
    all_to_all x1, blocking collectives, local(): kept = lax.all_to_all(ready, 'z', 0, 0)  10.7 us
    ppermute x3, starting transfers between devices, swap_cores(): return lax.ppermute(array, 'core', [(0, 1), (1, 0)])  8.99 us
    all_to_all x1, starting transfers between devices, local(): lax.all_to_all(partial.reshape(Z * C, 4 * CHZ, BS), ('z', 'core'), 0, 0)  8.59 us
    ppermute x2, starting transfers between devices, spread(): received = lax.ppermute(tie(array), 'z', SPREAD[step])  8 us
    unnamed x19, local copies, waits for them, and re-layouts  7.7 us
    pallas_call x1, Pallas kernels, field_partials(): pl.pallas_call(field_kernel, in_specs=[IN_SMEM] * 3 + [IN_VMEM] * 4, out_...  6.92 us
  transfers between devices with their start and end apart: 18, of which 11 were waited for; matrix products, arithmetic and copies ran while one was open for 6% of the time, Pallas kernels for 12%

profile of v4, /device:TPU:1, one launch (start us, length us, event | category | flops | bytes accessed | tf_op | source)
XLA Modules:
  0.0 120.0 jit_solution(13705425111873990016)
XLA Ops:
  0.0 2.1 %collective-permute-start.3 = (bf16[8,64,512]{2,1,0:T(8,128)(2,1)}, bf16[8,64,512]{2,1,0:T(8,128)(2,1)S(1)}, u32[]{:S(2)}, u32[]{:S(2)}) collective-permute-start(bf16[8,64,512]{2,1,0:T(8,128)(2,1)} %param.6), channel_id=1, source_target_pairs={{0,16},{1,65},{2,18},{3,67},{4,20},{5,69},{6,22},{7,71},{8,24},{9,... | collective-permute-start | bytes 1572872 | tf_op jit(solution)/shard_map/ppermute | solution.py:42
  2.1 1.5 %collective-permute-start.2 = (bf16[8,64,512]{2,1,0:T(8,128)(2,1)}, bf16[8,64,512]{2,1,0:T(8,128)(2,1)S(1)}, u32[]{:S(2)}, u32[]{:S(2)}) collective-permute-start(bf16[8,64,512]{2,1,0:T(8,128)(2,1)} %param.6), channel_id=1, source_target_pairs={{0,48},{1,193},{2,50},{3,195},{4,52},{5,197},{6,54},{7,199},{8,56}... | collective-permute-start | bytes 1572872 | tf_op jit(solution)/shard_map/ppermute | solution.py:42
  3.7 3.1 %packed_front.1 = bf16[2,2064,128]{2,1,0:T(8,128)(2,1)} custom-call(bf16[32768,128]{1,0:T(8,128)(2,1)} %bitcast.31, s32[8,4,8]{2,1,0:T(4,128)} %pattern_ref.1), custom_call_target="tpu_custom_call" | custom-call | tf_op jit(solution)/shard_map/packed_front/pallas_call | solution.py:83
  6.8 2.8 %collective-permute-start = (bf16[2,2064,128]{2,1,0:T(8,128)(2,1)}, bf16[2,2064,128]{2,1,0:T(8,128)(2,1)S(1)}, u32[]{:S(2)}, u32[]{:S(2)}) collective-permute-start(bf16[2,2064,128]{2,1,0:T(8,128)(2,1)} %packed_front.1), channel_id=1, source_target_pairs={{0,15},{1,0},{2,1},{3,2},{4,3},{5,4},{6,5},{7,6},{8,7},{9,8},{10,9... | collective-permute-start | bytes 3170312 | tf_op jit(solution)/shard_map/ppermute | solution.py:278
  9.7 1.0 collective-permute-done.3
  10.6 0.7 slice.41
  11.5 0.1 add.153
  11.6 2.7 %collective-permute-start.5 = (bf16[4,64,512]{2,1,0:T(8,128)(2,1)S(1)}, bf16[4,64,512]{2,1,0:T(8,128)(2,1)S(1)}, u32[]{:S(2)}, u32[]{:S(2)}) collective-permute-start(bf16[4,64,512]{2,1,0:T(8,128)(2,1)S(1)} %slice.42), channel_id=1, source_target_pairs={{0,48},{1,193},{2,50},{3,195},{4,52},{5,197},{6,54},{7,199},{8,56}... | collective-permute-start | bytes 786440 | tf_op jit(solution)/shard_map/ppermute | solution.py:42
  14.4 1.0 collective-permute-start.7
  15.4 1.1 constant_dynamic-update-slice_fusion.2
  16.5 1.6 %collective-permute-done.4 = bf16[4,64,512]{2,1,0:T(8,128)(2,1)} collective-permute-done((bf16[4,64,512]{2,1,0:T(8,128)(2,1)}, bf16[4,64,512]{2,1,0:T(8,128)(2,1)}, u32[]{:S(2)}, u32[]{:S(2)}) %collective-permute-start.4) | collective-permute-done | bytes 262176 | tf_op jit(solution)/shard_map/ppermute | solution.py:42
  18.1 1.0 constant_dynamic-update-slice_fusion.1
  19.1 2.6 %collective-permute-start.11 = (bf16[16,64,512]{2,1,0:T(8,128)(2,1)S(1)}, bf16[16,64,512]{2,1,0:T(8,128)(2,1)}, u32[]{:S(2)}, u32[]{:S(2)}) collective-permute-start(bf16[16,64,512]{2,1,0:T(8,128)(2,1)S(1)} %constant_dynamic-update-slice_fusion.refs_1_), channel_id=1, source_target_pairs={{0,192},{1,49},{2,194},{3,51},{4,196},{5,53},{6,198},{7,55},{8,200... | collective-permute-start | bytes 3145736 | tf_op jit(solution)/shard_map/ppermute | solution.py:42
  21.7 0.1 fusion.9
  21.8 0.1 reshape.57.now_idx
  21.9 0.7 collective-permute-done.next_ref
  22.6 1.1 fusion.2
  23.7 6.2 %collective-permute-start.1 = (bf16[2064,128]{1,0:T(8,128)(2,1)S(1)}, bf16[2064,128]{1,0:T(8,128)(2,1)S(1)}, u32[]{:S(2)}, u32[]{:S(2)}) collective-permute-start(bf16[2064,128]{1,0:T(8,128)(2,1)S(1)} %fusion.2), channel_id=1, source_target_pairs={{0,1},{1,0},{2,3},{3,2},{4,5},{5,4},{6,7},{7,6},{8,9},{9,8},{10,11... | collective-permute-start | bytes 1585160 | tf_op jit(solution)/shard_map/ppermute | solution.py:24
  29.9 2.7 %collective-permute-done.7.refs_2_ = bf16[16,64,512]{2,1,0:T(8,128)(2,1)} collective-permute-done((bf16[16,64,512]{2,1,0:T(8,128)(2,1)S(1)}, bf16[16,64,512]{2,1,0:T(8,128)(2,1)}, u32[]{:S(2)}, u32[]{:S(2)}) %collective-permute-start.7) | collective-permute-done | bytes 1048608 | tf_op jit(solution)/shard_map/ppermute | solution.py:42
  32.6 1.0 collective-permute-start.8
  33.6 0.6 collective-permute-start.12
  34.2 2.8 %collective-permute-start.13 = (bf16[16,64,512]{2,1,0:T(8,128)(2,1)}, bf16[16,64,512]{2,1,0:T(8,128)(2,1)}, u32[]{:S(2)}, u32[]{:S(2)}) collective-permute-start(bf16[16,64,512]{2,1,0:T(8,128)(2,1)} %collective-permute-done.11.refs_5_), channel_id=1, source_target_pairs={{0,192},{1,49},{2,194},{3,51},{4,196},{5,53},{6,198},{7,55},{8,200... | collective-permute-start | bytes 3145736 | tf_op jit(solution)/shard_map/ppermute | solution.py:42
  36.9 0.9 fusion.1
  37.8 6.0 %collective-permute-done.6.refs_3_ = bf16[16,64,512]{2,1,0:T(8,128)(2,1)} collective-permute-done((bf16[16,64,512]{2,1,0:T(8,128)(2,1)S(1)}, bf16[16,64,512]{2,1,0:T(8,128)(2,1)}, u32[]{:S(2)}, u32[]{:S(2)}) %collective-permute-start.6) | collective-permute-done | bytes 1048608 | tf_op jit(solution)/shard_map/ppermute | solution.py:42
  43.8 2.8 %collective-permute-done.8.refs_4_ = bf16[16,64,512]{2,1,0:T(8,128)(2,1)S(1)} collective-permute-done((bf16[16,64,512]{2,1,0:T(8,128)(2,1)S(1)}, bf16[16,64,512]{2,1,0:T(8,128)(2,1)S(1)}, u32[]{:S(2)}, u32[]{:S(2)}) %collective-permute-start.8) | collective-permute-done | bytes 1048608 | tf_op jit(solution)/shard_map/ppermute | solution.py:42
  46.6 1.0 copy-done.2
  47.6 4.7 %collective-permute-start.9 = (bf16[2064,128]{1,0:T(8,128)(2,1)}, bf16[2064,128]{1,0:T(8,128)(2,1)}, u32[]{:S(2)}, u32[]{:S(2)}) collective-permute-start(bf16[2064,128]{1,0:T(8,128)(2,1)} %fusion.1), channel_id=1, source_target_pairs={{0,4},{14,10},{1,5},{15,11},{16,20},{30,26},{17,21},{31,27},{32,36... | collective-permute-start | bytes 1585160 | tf_op jit(solution)/shard_map/ppermute | solution.py:256
  52.3 0.1 concatenate.15
  52.4 2.6 %collective-permute-done.12.refs_6_ = bf16[16,64,512]{2,1,0:T(8,128)(2,1)} collective-permute-done((bf16[16,64,512]{2,1,0:T(8,128)(2,1)}, bf16[16,64,512]{2,1,0:T(8,128)(2,1)}, u32[]{:S(2)}, u32[]{:S(2)}) %collective-permute-start.12) | collective-permute-done | bytes 1048608 | tf_op jit(solution)/shard_map/ppermute | solution.py:42
  55.0 3.4 %copy-done.1 = bf16[8,4,8,128,128]{4,3,2,1,0:T(8,128)(2,1)S(1)} copy-done((bf16[8,4,8,128,128]{4,3,2,1,0:T(8,128)(2,1)S(1)}, bf16[8,4,8,128,128]{4,3,2,1,0:T(8,128)(2,1)}, u32[]{:S(2)}) %copy-start.1) | copy-done | bytes 8388632
  58.4 1.2 %copy-done.3 = bf16[16,64,512]{2,1,0:T(8,128)(2,1)S(1)} copy-done((bf16[16,64,512]{2,1,0:T(8,128)(2,1)S(1)}, bf16[16,64,512]{2,1,0:T(8,128)(2,1)}, u32[]{:S(2)}) %copy-start.3) | copy-done | bytes 1048600
  59.7 3.0 %staged.1 = (bf16[112,64,512]{2,1,0:T(8,128)(2,1)S(1)}, bf16[8,4,8,128,128]{4,3,2,1,0:T(8,128)(2,1)S(1)}) custom-call(bf16[8,4,8,128,128]{4,3,2,1,0:T(8,128)(2,1)S(1)} %copy-done.1, bf16[16,64,512]{2,1,0:T(8,128)(2,1)S(1)} %constant_dynamic-update-slice_fusion.3.refs_0_, bf16[16,64,512]{2,1,0:T(8,128)(2,1)S(1)} %constant_dynamic-update-slice_fusion.refs_1_, ...), custom_call_target="tpu_custom_call" | custom-call | bytes 16777216 | tf_op jit(solution)/shard_map/staged/pallas_call | solution.py:158
  62.7 6.9 %field_partials.1 = f32[8,2,2,2,8,128]{5,4,3,2,1,0:T(8,128)} custom-call(s32[256]{0:T(256)S(1)} %reshape.57.now_idx, s32[256]{0:T(256)S(1)} %fusion.11.past_idx, s32[1]{0:T(128)} %bitcast.5.is_last, bf16[8,4,8,128,128]{4,3,2,1,0:T(8,128)(2,1)S(1)} %get-tuple-element.16.squares, bf16[2,2064,128]{2,1,0:T(8,128)(2,1)S(1)} %collective-permute-done.next_ref, ...), custom_call_target="tpu_custom_call" | custom-call | flops 1073741824 | bytes 16777216 | tf_op jit(solution)/shard_map/field_partials/pallas_call | solution.py:174
  69.6 8.6 %all-to-all-start = ((f32[16,32,128]{2,1,0:T(8,128)}), f32[16,32,128]{2,1,0:T(8,128)S(1)}, u32[]{:S(2)}, u32[]{:S(2)}) async-start(f32[16,32,128]{2,1,0:T(8,128)} %bitcast.6), calls=%async_computation | async-start | bytes 524288 | tf_op jit(solution)/shard_map/all_to_all | solution.py:292
  78.2 1.1 broadcast_select_fusion
  79.3 3.3 %collective-permute-start.10 = (bf16[2064,128]{1,0:T(8,128)(2,1)S(1)}, bf16[2064,128]{1,0:T(8,128)(2,1)S(1)}, u32[]{:S(2)}, u32[]{:S(2)}) collective-permute-start(bf16[2064,128]{1,0:T(8,128)(2,1)S(1)} %broadcast_select_fusion), channel_id=1, source_target_pairs={{0,2},{4,6},{10,8},{14,12},{1,3},{5,7},{11,9},{15,13},{16,18},{20,... | collective-permute-start | bytes 1585160 | tf_op jit(solution)/shard_map/ppermute | solution.py:256
  82.7 0.7 dynamic-slice_bitcast_fusion.excite_ref
  83.4 6.5 %all-to-all-done.parts_ref = f32[16,32,128]{2,1,0:T(8,128)S(1)} async-done(((f32[16,32,128]{2,1,0:T(8,128)}), f32[16,32,128]{2,1,0:T(8,128)S(1)}, u32[]{:S(2)}, u32[]{:S(2)}) %all-to-all-start) | async-done | bytes 262176 | tf_op jit(solution)/shard_map/all_to_all | solution.py:292
  89.9 1.0 first_solve.1
  90.9 4.8 %all-to-all-start.1 = ((bf16[16,16,128]{2,1,0:T(8,128)(2,1)}), bf16[16,16,128]{2,1,0:T(8,128)(2,1)S(1)}, u32[]{:S(2)}, u32[]{:S(2)}) async-start(bf16[16,16,128]{2,1,0:T(8,128)(2,1)} %get-tuple-element.18), calls=%async_computation.1 | async-start | bytes 131072 | tf_op jit(solution)/shard_map/all_to_all | solution.py:300
  95.7 6.8 %all-to-all-done.1.mine_ref = bf16[16,16,128]{2,1,0:T(8,128)(2,1)S(1)} async-done(((bf16[16,16,128]{2,1,0:T(8,128)(2,1)}), bf16[16,16,128]{2,1,0:T(8,128)(2,1)S(1)}, u32[]{:S(2)}, u32[]{:S(2)}) %all-to-all-start.1) | async-done | bytes 65568 | tf_op jit(solution)/shard_map/all_to_all | solution.py:300
  102.5 0.7 collective-permute-start.14
  103.4 0.7 collective-permute-done.14.other_ref
  104.1 1.3 %second_solve.1 = f32[8,2,16,128]{3,2,1,0:T(8,128)S(1)} custom-call(s32[16]{0:T(128)S(1)} %fusion.16.idx, bf16[16,16,128]{2,1,0:T(8,128)(2,1)S(1)} %all-to-all-done.1.mine_ref, bf16[16,16,128]{2,1,0:T(8,128)(2,1)S(1)} %collective-permute-done.14.other_ref, bf16[2064,128]{1,0:T(8,128)(2,1)S(1)} %broadcast_select_fusion.1.blocks_ref, ...), custom_call_target="tpu_custom_call" | custom-call | tf_op jit(solution)/shard_map/second_solve/pallas_call | solution.py:240
  105.4 10.7 %all_to_all.15 = f32[8,2,16,128]{3,2,1,0:T(8,128)S(1)} all-to-all(f32[8,2,16,128]{3,2,1,0:T(8,128)S(1)} %second_solve.1), channel_id=1, replica_groups=mesh['y'=4,'x'=4,'z'=8,'core'=2] {'z'}, dimensions={0} | all-to-all | bytes 262144 | tf_op jit(solution)/shard_map/all_to_all | solution.py:306
  116.1 2.1 %collective-permute-start.15 = (f32[8,2,16,128]{3,2,1,0:T(8,128)S(1)}, f32[8,2,16,128]{3,2,1,0:T(8,128)S(1)}, u32[]{:S(2)}, u32[]{:S(2)}) collective-permute-start(f32[8,2,16,128]{3,2,1,0:T(8,128)S(1)} %all_to_all.15), channel_id=1, source_target_pairs={{0,1},{1,0},{2,3},{3,2},{4,5},{5,4},{6,7},{7,6},{8,9},{9,8},{10,11... | collective-permute-start | bytes 393224 | tf_op jit(solution)/shard_map/ppermute | solution.py:24
  118.2 1.0 collective-permute-done.15
  119.3 0.7 copy.6
  (42 shorter events, 0.6 us)
Async XLA Ops:
  0.0 83.4 %copy-start = (f32[4,128,128]{2,1,0:T(8,128)S(1)}, f32[4,128,128]{2,1,0:T(8,128)}, u32[]{:S(2)}) copy-start(f32[4,128,128]{2,1,0:T(8,128)} %param.9) | copy-start | bytes 786436
  0.0 10.6 %collective-permute-start.3 = (bf16[8,64,512]{2,1,0:T(8,128)(2,1)}, bf16[8,64,512]{2,1,0:T(8,128)(2,1)S(1)}, u32[]{:S(2)}, u32[]{:S(2)}) collective-permute-start(bf16[8,64,512]{2,1,0:T(8,128)(2,1)} %param.6), channel_id=1, source_target_pairs={{0,16},{1,65},{2,18},{3,67},{4,20},{5,69},{6,22},{7,71},{8,24},{9,... | collective-permute-start | bytes 1572872 | tf_op jit(solution)/shard_map/ppermute | solution.py:42
  2.1 9.5 %collective-permute-start.2 = (bf16[8,64,512]{2,1,0:T(8,128)(2,1)}, bf16[8,64,512]{2,1,0:T(8,128)(2,1)S(1)}, u32[]{:S(2)}, u32[]{:S(2)}) collective-permute-start(bf16[8,64,512]{2,1,0:T(8,128)(2,1)} %param.6), channel_id=1, source_target_pairs={{0,48},{1,193},{2,50},{3,195},{4,52},{5,197},{6,54},{7,199},{8,56}... | collective-permute-start | bytes 1572872 | tf_op jit(solution)/shard_map/ppermute | solution.py:42
  3.7 6.0 %copy-start.6 = (bf16[8,64,512]{2,1,0:T(8,128)(2,1)S(1)}, bf16[8,64,512]{2,1,0:T(8,128)(2,1)}, u32[]{:S(2)}) copy-start(bf16[8,64,512]{2,1,0:T(8,128)(2,1)} %param.6) | copy-start | bytes 1572868
  6.8 15.8 %collective-permute-start = (bf16[2,2064,128]{2,1,0:T(8,128)(2,1)}, bf16[2,2064,128]{2,1,0:T(8,128)(2,1)S(1)}, u32[]{:S(2)}, u32[]{:S(2)}) collective-permute-start(bf16[2,2064,128]{2,1,0:T(8,128)(2,1)} %packed_front.1), channel_id=1, source_target_pairs={{0,15},{1,0},{2,1},{3,2},{4,3},{5,4},{6,5},{7,6},{8,7},{9,8},{10,9... | collective-permute-start | bytes 3170312 | tf_op jit(solution)/shard_map/ppermute | solution.py:278
  11.4 6.7 %collective-permute-start.4 = (bf16[4,64,512]{2,1,0:T(8,128)(2,1)}, bf16[4,64,512]{2,1,0:T(8,128)(2,1)}, u32[]{:S(2)}, u32[]{:S(2)}) collective-permute-start(bf16[4,64,512]{2,1,0:T(8,128)(2,1)} %slice.41), channel_id=1, source_target_pairs={{0,16},{1,65},{2,18},{3,67},{4,20},{5,69},{6,22},{7,71},{8,24},{9,... | collective-permute-start | bytes 786440 | tf_op jit(solution)/shard_map/ppermute | solution.py:42
  11.6 2.8 %copy-start.5 = (bf16[8,64,512]{2,1,0:T(8,128)(2,1)}, bf16[8,64,512]{2,1,0:T(8,128)(2,1)S(1)}, u32[]{:S(2)}) copy-start(bf16[8,64,512]{2,1,0:T(8,128)(2,1)S(1)} %collective-permute-done.2) | copy-start | bytes 1572868
  11.6 7.4 %collective-permute-start.5 = (bf16[4,64,512]{2,1,0:T(8,128)(2,1)S(1)}, bf16[4,64,512]{2,1,0:T(8,128)(2,1)S(1)}, u32[]{:S(2)}, u32[]{:S(2)}) collective-permute-start(bf16[4,64,512]{2,1,0:T(8,128)(2,1)S(1)} %slice.42), channel_id=1, source_target_pairs={{0,48},{1,193},{2,50},{3,195},{4,52},{5,197},{6,54},{7,199},{8,56}... | collective-permute-start | bytes 786440 | tf_op jit(solution)/shard_map/ppermute | solution.py:42
  14.4 7.3 %copy-start.7 = (s32[8,4,8]{2,1,0:T(4,128)S(1)}, s32[8,4,8]{2,1,0:T(4,128)}, u32[]{:S(2)}) copy-start(s32[8,4,8]{2,1,0:T(4,128)} %pattern_ref.1) | copy-start | bytes 3076
  14.4 18.1 %collective-permute-start.7 = (bf16[16,64,512]{2,1,0:T(8,128)(2,1)S(1)}, bf16[16,64,512]{2,1,0:T(8,128)(2,1)}, u32[]{:S(2)}, u32[]{:S(2)}) collective-permute-start(bf16[16,64,512]{2,1,0:T(8,128)(2,1)S(1)} %constant_dynamic-update-slice_fusion.3.refs_0_), channel_id=1, source_target_pairs={{0,64},{1,17},{2,66},{3,19},{4,68},{5,21},{6,70},{7,23},{8,72},{9,... | collective-permute-start | bytes 3145736 | tf_op jit(solution)/shard_map/ppermute | solution.py:42
  19.1 15.1 %collective-permute-start.11 = (bf16[16,64,512]{2,1,0:T(8,128)(2,1)S(1)}, bf16[16,64,512]{2,1,0:T(8,128)(2,1)}, u32[]{:S(2)}, u32[]{:S(2)}) collective-permute-start(bf16[16,64,512]{2,1,0:T(8,128)(2,1)S(1)} %constant_dynamic-update-slice_fusion.refs_1_), channel_id=1, source_target_pairs={{0,192},{1,49},{2,194},{3,51},{4,196},{5,53},{6,198},{7,55},{8,200... | collective-permute-start | bytes 3145736 | tf_op jit(solution)/shard_map/ppermute | solution.py:42
  21.7 22.1 %collective-permute-start.6 = (bf16[16,64,512]{2,1,0:T(8,128)(2,1)S(1)}, bf16[16,64,512]{2,1,0:T(8,128)(2,1)}, u32[]{:S(2)}, u32[]{:S(2)}) collective-permute-start(bf16[16,64,512]{2,1,0:T(8,128)(2,1)S(1)} %constant_dynamic-update-slice_fusion.refs_1_), channel_id=1, source_target_pairs={{0,64},{1,17},{2,66},{3,19},{4,68},{5,21},{6,70},{7,23},{8,72},{9,... | collective-permute-start | bytes 3145736 | tf_op jit(solution)/shard_map/ppermute | solution.py:42
  21.9 15.1 %copy-start.4 = (bf16[2,2064,128]{2,1,0:T(8,128)(2,1)S(1)}, bf16[2,2064,128]{2,1,0:T(8,128)(2,1)}, u32[]{:S(2)}) copy-start(bf16[2,2064,128]{2,1,0:T(8,128)(2,1)} %packed_front.1) | copy-start | bytes 3170308
  23.7 13.2 %collective-permute-start.1 = (bf16[2064,128]{1,0:T(8,128)(2,1)S(1)}, bf16[2064,128]{1,0:T(8,128)(2,1)S(1)}, u32[]{:S(2)}, u32[]{:S(2)}) collective-permute-start(bf16[2064,128]{1,0:T(8,128)(2,1)S(1)} %fusion.2), channel_id=1, source_target_pairs={{0,1},{1,0},{2,3},{3,2},{4,5},{5,4},{6,7},{7,6},{8,9},{9,8},{10,11... | collective-permute-start | bytes 1585160 | tf_op jit(solution)/shard_map/ppermute | solution.py:24
  32.6 14.0 %collective-permute-start.8 = (bf16[16,64,512]{2,1,0:T(8,128)(2,1)S(1)}, bf16[16,64,512]{2,1,0:T(8,128)(2,1)S(1)}, u32[]{:S(2)}, u32[]{:S(2)}) collective-permute-start(bf16[16,64,512]{2,1,0:T(8,128)(2,1)S(1)} %constant_dynamic-update-slice_fusion.3.refs_0_), channel_id=1, source_target_pairs={{0,192},{1,49},{2,194},{3,51},{4,196},{5,53},{6,198},{7,55},{8,200... | collective-permute-start | bytes 3145736 | tf_op jit(solution)/shard_map/ppermute | solution.py:42
  33.6 18.7 %slice-start = ((s32[8,4,8]{2,1,0:T(4,128)}), s32[7,4,8]{2,1,0:T(4,128)S(1)}, s32[]{:S(2)}) async-start(s32[8,4,8]{2,1,0:T(4,128)} %pattern_ref.1), calls=%async_computation.3 | async-start | bytes 28672 | tf_op jit(solution)/shard_map/slice | solution.py:287
  33.6 21.4 %collective-permute-start.12 = (bf16[16,64,512]{2,1,0:T(8,128)(2,1)}, bf16[16,64,512]{2,1,0:T(8,128)(2,1)}, u32[]{:S(2)}, u32[]{:S(2)}) collective-permute-start(bf16[16,64,512]{2,1,0:T(8,128)(2,1)} %collective-permute-done.7.refs_2_), channel_id=1, source_target_pairs={{0,64},{1,17},{2,66},{3,19},{4,68},{5,21},{6,70},{7,23},{8,72},{9,... | collective-permute-start | bytes 3145736 | tf_op jit(solution)/shard_map/ppermute | solution.py:42
  34.2 28.5 %collective-permute-start.13 = (bf16[16,64,512]{2,1,0:T(8,128)(2,1)}, bf16[16,64,512]{2,1,0:T(8,128)(2,1)}, u32[]{:S(2)}, u32[]{:S(2)}) collective-permute-start(bf16[16,64,512]{2,1,0:T(8,128)(2,1)} %collective-permute-done.11.refs_5_), channel_id=1, source_target_pairs={{0,192},{1,49},{2,194},{3,51},{4,196},{5,53},{6,198},{7,55},{8,200... | collective-permute-start | bytes 3145736 | tf_op jit(solution)/shard_map/ppermute | solution.py:42
  46.6 1.0 copy-start.2
  47.6 30.6 %collective-permute-start.9 = (bf16[2064,128]{1,0:T(8,128)(2,1)}, bf16[2064,128]{1,0:T(8,128)(2,1)}, u32[]{:S(2)}, u32[]{:S(2)}) collective-permute-start(bf16[2064,128]{1,0:T(8,128)(2,1)} %fusion.1), channel_id=1, source_target_pairs={{0,4},{14,10},{1,5},{15,11},{16,20},{30,26},{17,21},{31,27},{32,36... | collective-permute-start | bytes 1585160 | tf_op jit(solution)/shard_map/ppermute | solution.py:256
  55.0 3.4 %copy-start.1 = (bf16[8,4,8,128,128]{4,3,2,1,0:T(8,128)(2,1)S(1)}, bf16[8,4,8,128,128]{4,3,2,1,0:T(8,128)(2,1)}, u32[]{:S(2)}) copy-start(bf16[8,4,8,128,128]{4,3,2,1,0:T(8,128)(2,1)} %blocks_ref.1) | copy-start | bytes 25165828
  58.4 1.2 %copy-start.3 = (bf16[16,64,512]{2,1,0:T(8,128)(2,1)S(1)}, bf16[16,64,512]{2,1,0:T(8,128)(2,1)}, u32[]{:S(2)}) copy-start(bf16[16,64,512]{2,1,0:T(8,128)(2,1)} %copy-done.2) | copy-start | bytes 3145732
  69.6 20.3 %all-to-all-start = ((f32[16,32,128]{2,1,0:T(8,128)}), f32[16,32,128]{2,1,0:T(8,128)S(1)}, u32[]{:S(2)}, u32[]{:S(2)}) async-start(f32[16,32,128]{2,1,0:T(8,128)} %bitcast.6), calls=%async_computation | async-start | bytes 524288 | tf_op jit(solution)/shard_map/all_to_all | solution.py:292
  79.3 23.9 %collective-permute-start.10 = (bf16[2064,128]{1,0:T(8,128)(2,1)S(1)}, bf16[2064,128]{1,0:T(8,128)(2,1)S(1)}, u32[]{:S(2)}, u32[]{:S(2)}) collective-permute-start(bf16[2064,128]{1,0:T(8,128)(2,1)S(1)} %broadcast_select_fusion), channel_id=1, source_target_pairs={{0,2},{4,6},{10,8},{14,12},{1,3},{5,7},{11,9},{15,13},{16,18},{20,... | collective-permute-start | bytes 1585160 | tf_op jit(solution)/shard_map/ppermute | solution.py:256
  90.9 11.6 %all-to-all-start.1 = ((bf16[16,16,128]{2,1,0:T(8,128)(2,1)}), bf16[16,16,128]{2,1,0:T(8,128)(2,1)S(1)}, u32[]{:S(2)}, u32[]{:S(2)}) async-start(bf16[16,16,128]{2,1,0:T(8,128)(2,1)} %get-tuple-element.18), calls=%async_computation.1 | async-start | bytes 131072 | tf_op jit(solution)/shard_map/all_to_all | solution.py:300
  102.5 1.6 %collective-permute-start.14 = (bf16[16,16,128]{2,1,0:T(8,128)(2,1)S(1)}, bf16[16,16,128]{2,1,0:T(8,128)(2,1)S(1)}, u32[]{:S(2)}, u32[]{:S(2)}) collective-permute-start(bf16[16,16,128]{2,1,0:T(8,128)(2,1)S(1)} %all-to-all-done.1.mine_ref), channel_id=1, source_target_pairs={{0,1},{1,0},{2,3},{3,2},{4,5},{5,4},{6,7},{7,6},{8,9},{9,8},{10,11... | collective-permute-start | bytes 196616 | tf_op jit(solution)/shard_map/ppermute | solution.py:24
  116.1 3.1 %collective-permute-start.15 = (f32[8,2,16,128]{3,2,1,0:T(8,128)S(1)}, f32[8,2,16,128]{3,2,1,0:T(8,128)S(1)}, u32[]{:S(2)}, u32[]{:S(2)}) collective-permute-start(f32[8,2,16,128]{3,2,1,0:T(8,128)S(1)} %all_to_all.15), channel_id=1, source_target_pairs={{0,1},{1,0},{2,3},{3,2},{4,5},{5,4},{6,7},{7,6},{8,9},{9,8},{10,11... | collective-permute-start | bytes 393224 | tf_op jit(solution)/shard_map/ppermute | solution.py:24
